TPU v7x, 256 devices: a whole 4x4x8 slice. The times are simulated.
256 devices in a mesh: section: 8 (over z), expert: 32 (over y, x, core).
Axes of the slice: x: 4, y: 4, z: 8, core: 2. Of those that a mesh axis runs over, the one named last changes fastest.
Arguments:
- fwd_input: bfloat16 [8, 3072, 7168], P('section', 'expert'), may hold values from -6 to 6
- saved_input: bfloat16 [8, 3072, 7168], P('section', 'expert'), may hold values from -6 to 6
- out_cotangent: bfloat16 [8, 3072, 7168], P('section', 'expert'), may hold values from -6 to 6
- fwd_routes: int32 [8, 3072, 8], P('section', 'expert'), may hold values from 0 to 255, as said below
- bwd_routes: int32 [8, 3072, 8], P('section', 'expert'), may hold values from 0 to 255, as said below
- fwd_scores: float32 [8, 3072, 8], P('section', 'expert'), may hold values from -6 to 6
- bwd_scores: float32 [8, 3072, 8], P('section', 'expert'), may hold values from -6 to 6
- norm_gain: float32 [8, 7168], P('section'), may hold values from 0.1 to 1.9
- gate_proj: bfloat16 [8, 32, 7168, 128], P('section', 'expert'), may hold values from -0.0625 to 0.0625
- up_proj: bfloat16 [8, 32, 7168, 128], P('section', 'expert'), may hold values from -0.0625 to 0.0625
- down_proj: bfloat16 [8, 32, 128, 7168], P('section', 'expert'), may hold values from -0.1875 to 0.1875
Outputs:
- fwd_handoff: bfloat16 [8, 3072, 7168], P('section', 'expert')
- grad_handoff: bfloat16 [8, 3072, 7168], P('section', 'expert')
- score_grads: float32 [8, 3072, 8], P('section', 'expert')
Inputs may be any that keep to these rules, and one draw needn't show every extreme that they name: `fwd_routes`: each row names 8 different experts. Among the rows of one device, no expert below 4 is named by more than 8 rows, and in every section one expert below 4 is named by exactly 8 rows of every device. `bwd_routes`: as for fwd_routes.
All inputs are finite; a program needn't handle non-finite values.
Results may differ from a plain program's by a relative error of at most 0.017.
Values may be sent and summed in bfloat16 or wider, within the bound.
No kernel may reach another device: no remote copies, remote signals or barrier semaphores. Data moves between devices by JAX's collectives and lax.ppermute only.
A program may use at most 128 MiB of HBM per device.

v0:
```python
import jax
import jax.numpy as jnp
from jax import lax
from jax.sharding import PartitionSpec as P

GROUP = 8
CAP = 8


EPSILON = 1e-06
ROUTE_SCALE = 2.5


def shifted(array, axis, by):
    size = lax.axis_size(axis)
    return lax.ppermute(array, axis, [(i, (i + by) % size) for i in range(size)])


def normalize(values, gain_row):
    inverse = lax.rsqrt(jnp.mean(values * values, axis=-1, keepdims=True) + EPSILON)
    return (values * inverse * gain_row, inverse)


def route_tables(routes, scores, window, capacity):
    affinity = jax.nn.sigmoid(scores)
    aff_total = jnp.sum(affinity, axis=-1, keepdims=True)
    gate_vals = ROUTE_SCALE * affinity / aff_total
    expert_ids = jnp.arange(window, dtype=jnp.int32)
    matches = (routes[:, :, None] == expert_ids[None, None, :]).astype(jnp.float32)
    naming = jnp.sum(matches, axis=1)
    earlier = jnp.cumsum(naming, axis=0) - naming
    slot_ids = jnp.arange(capacity, dtype=jnp.float32)
    table = naming.T[:, None, :] * (earlier.T[:, None, :] == slot_ids[None, :, None]).astype(
        jnp.float32
    )
    route_weight = jnp.sum(matches * gate_vals[:, :, None], axis=1)
    mixing = table * route_weight.T[:, None, :]
    return (affinity, aff_total, gate_vals, matches, table, mixing)


def slice_forward(inputs, w_gate, w_up, w_down):
    pre_gate = jnp.dot(inputs, w_gate, preferred_element_type=jnp.float32)
    pre_up = jnp.dot(inputs, w_up, preferred_element_type=jnp.float32)
    hidden = (pre_gate * jax.nn.sigmoid(pre_gate) * pre_up).astype(jnp.bfloat16)
    return jnp.dot(hidden, w_down, preferred_element_type=jnp.float32).astype(jnp.bfloat16)


def slice_backward(inputs, cotangent, w_gate, w_up, w_down):
    pre_gate = jnp.dot(inputs, w_gate, preferred_element_type=jnp.float32)
    pre_up = jnp.dot(inputs, w_up, preferred_element_type=jnp.float32)
    gate_sig = jax.nn.sigmoid(pre_gate)
    active = pre_gate * gate_sig
    hidden = (active * pre_up).astype(jnp.bfloat16)
    partial_value = jnp.dot(hidden, w_down, preferred_element_type=jnp.float32).astype(jnp.bfloat16)
    d_hidden = jnp.dot(cotangent, w_down.T, preferred_element_type=jnp.float32)
    d_gate = (d_hidden * pre_up * gate_sig * (1.0 + pre_gate * (1.0 - gate_sig))).astype(
        jnp.bfloat16
    )
    d_up = (d_hidden * active).astype(jnp.bfloat16)
    d_input = (
        jnp.dot(d_gate, w_gate.T, preferred_element_type=jnp.float32)
        + jnp.dot(d_up, w_up.T, preferred_element_type=jnp.float32)
    ).astype(jnp.bfloat16)
    return (d_input, partial_value)


def gather_slots(table, normed):
    return jnp.einsum(
        "wcr,rd->wcd", table.astype(jnp.bfloat16), normed, preferred_element_type=jnp.float32
    ).astype(jnp.bfloat16)


def per_device(
    fwd_input,
    saved_input,
    out_cotangent,
    fwd_routes,
    bwd_routes,
    fwd_scores,
    bwd_scores,
    norm_gain,
    gate_proj,
    up_proj,
    down_proj,
):
    highest = lax.Precision.HIGHEST
    group_size = GROUP
    capacity = CAP
    devices = lax.axis_size("expert")
    window = devices // group_size
    width = fwd_input.shape[2]
    gate_slice = gate_proj[0, 0]
    up_slice = up_proj[0, 0]
    down_slice = down_proj[0, 0]
    gain_row = norm_gain[0]
    x_fwd = fwd_input[0].astype(jnp.float32)
    normed_f = normalize(x_fwd, gain_row)[0].astype(jnp.bfloat16)
    tab_f = route_tables(fwd_routes[0], fwd_scores[0], window, capacity)
    slots_f = gather_slots(tab_f[4], normed_f)
    x_bwd = saved_input[0].astype(jnp.float32)
    cot_rows = out_cotangent[0]
    normed_b, inverse_b = normalize(x_bwd, gain_row)
    normed_b = normed_b.astype(jnp.bfloat16)
    affinity, aff_total, gate_vals, matches, table_b, mixing_b = route_tables(
        bwd_routes[0], bwd_scores[0], window, capacity
    )
    slots_b = gather_slots(table_b, normed_b)
    slots_c = gather_slots(table_b, cot_rows)
    send_f = jnp.broadcast_to(slots_f[:, None], (window, group_size, capacity, width)).reshape(
        devices, capacity, width
    )
    received = lax.all_to_all(send_f, "expert", split_axis=0, concat_axis=0, tiled=True)
    outputs = slice_forward(received.reshape(-1, width), gate_slice, up_slice, down_slice)
    back_f = lax.all_to_all(
        outputs.reshape(received.shape), "expert", split_axis=0, concat_axis=0, tiled=True
    )
    expert_out = jnp.sum(
        back_f.reshape(window, group_size, capacity, width).astype(jnp.float32), axis=1
    )
    send_rows = jnp.broadcast_to(slots_b[:, None], (window, group_size, capacity, width)).reshape(
        devices, capacity, width
    )
    send_cot = jnp.broadcast_to(slots_c[:, None], (window, group_size, capacity, width)).reshape(
        devices, capacity, width
    )
    received = (
        lax.all_to_all(send_rows, "expert", split_axis=0, concat_axis=0, tiled=True),
        lax.all_to_all(send_cot, "expert", split_axis=0, concat_axis=0, tiled=True),
    )
    received_rows = received[0]
    d_input, partial_value = slice_backward(
        received_rows.reshape(-1, width),
        received[1].reshape(-1, width),
        gate_slice,
        up_slice,
        down_slice,
    )
    d_input = d_input.reshape(received_rows.shape)
    partial_value = partial_value.reshape(received_rows.shape)
    first = d_input
    second = partial_value
    first, second = (
        lax.all_to_all(first, "expert", split_axis=0, concat_axis=0, tiled=True),
        lax.all_to_all(second, "expert", split_axis=0, concat_axis=0, tiled=True),
    )
    dn_sum = jnp.sum(first.reshape(window, group_size, capacity, width).astype(jnp.float32), axis=1)
    returned = jnp.sum(
        second.reshape((window, group_size, capacity) + second.shape[2:]).astype(jnp.float32),
        axis=1,
    )
    dot_vals = jnp.sum(slots_c.astype(jnp.float32) * returned, axis=-1)
    branch = jnp.einsum("wcr,wcd->rd", tab_f[5], expert_out, precision=highest)
    layer_out = (x_fwd + branch).astype(jnp.bfloat16)
    dnormed = jnp.einsum("wcr,wcd->rd", mixing_b, dn_sum, precision=highest)
    dgate_expert = jnp.einsum("wcr,wc->rw", table_b, dot_vals, precision=highest)
    dgate = jnp.sum(matches * dgate_expert[:, None, :], axis=2)
    spread_term = jnp.sum(dgate * gate_vals, axis=-1, keepdims=True) / ROUTE_SCALE
    score_rows = affinity * (1.0 - affinity) * (ROUTE_SCALE / aff_total) * (dgate - spread_term)
    scaled = dnormed * gain_row
    grad = (
        cot_rows.astype(jnp.float32)
        + inverse_b * scaled
        - x_bwd
        * inverse_b
        * inverse_b
        * inverse_b
        * jnp.mean(x_bwd * scaled, axis=-1, keepdims=True)
    )
    layer_grad = grad.astype(jnp.bfloat16)
    fwd_handoff = shifted(layer_out[None], "section", 1)
    grad_handoff = shifted(layer_grad[None], "section", -1)
    return (fwd_handoff, grad_handoff, score_rows[None])


def solution(mesh):
    in_specs = (
        P("section", "expert", None),
        P("section", "expert", None),
        P("section", "expert", None),
        P("section", "expert", None),
        P("section", "expert", None),
        P("section", "expert", None),
        P("section", "expert", None),
        P("section", None),
        P("section", "expert", None, None),
        P("section", "expert", None, None),
        P("section", "expert", None, None),
    )
    out_specs = (
        P("section", "expert", None),
        P("section", "expert", None),
        P("section", "expert", None),
    )
    return jax.shard_map(
        per_device, mesh=mesh, in_specs=in_specs, out_specs=out_specs, check_vma=False
    )
```

profile of v0, /device:TPU:6, one launch (start us, length us, event | category | flops | bytes accessed | tf_op | source)
XLA Modules:
  0.0 373.3 jit_solution(12311585499673218551)
XLA Ops:
  1.9 1.7 fusion.28
  3.6 1.8 convolution_convert_fusion.2
  5.9 50.6 %all_to_all.30 = bf16[32,8,7168]{2,1,0:T(8,128)(2,1)S(1)} all-to-all(bf16[32,8,7168]{2,1,0:T(8,128)(2,1)S(1)} %bitcast.145), channel_id=1, replica_groups=mesh['section'=8,'expert'=32] {'expert'}, dimensions={0} | all-to-all | bytes 7340032 | tf_op jit(solution)/shard_map/all_to_all | solution.py:127
  59.2 2.9 fusion.3
  62.1 7.2 %all-to-all-start.5 = ((bf16[32,8,7168]{2,1,0:T(8,128)(2,1)}), bf16[32,8,7168]{2,1,0:T(8,128)(2,1)}, u32[]{:S(2)}, u32[]{:S(2)}) async-start(bf16[32,8,7168]{2,1,0:T(8,128)(2,1)} %fusion.3), calls=%async_computation.5 | async-start | bytes 7340032 | tf_op jit(solution)/shard_map/all_to_all | solution.py:144
  71.5 1.4 bitcast_subtract_fusion.1
  72.9 1.5 copy.24
  75.4 2.0 convolution_convert_fusion.4
  77.4 34.5 %all-to-all-done.5 = bf16[32,8,7168]{2,1,0:T(8,128)(2,1)} async-done(((bf16[32,8,7168]{2,1,0:T(8,128)(2,1)}), bf16[32,8,7168]{2,1,0:T(8,128)(2,1)}, u32[]{:S(2)}, u32[]{:S(2)}) %all-to-all-start.5) | async-done | bytes 3670048 | tf_op jit(solution)/shard_map/all_to_all | solution.py:144
  111.9 3.3 broadcast_in_dim.10
  115.3 9.9 %all-to-all-start = ((bf16[32,8,7168]{2,1,0:T(8,128)(2,1)}), bf16[32,8,7168]{2,1,0:T(8,128)(2,1)}, u32[]{:S(2)}, u32[]{:S(2)}) async-start(bf16[32,8,7168]{2,1,0:T(8,128)(2,1)} %bitcast.143), calls=%async_computation | async-start | bytes 7340032 | tf_op jit(solution)/shard_map/all_to_all | solution.py:112
  125.2 2.8 convert_reduce_fusion
  129.1 38.7 %all-to-all-done = bf16[32,8,7168]{2,1,0:T(8,128)(2,1)} async-done(((bf16[32,8,7168]{2,1,0:T(8,128)(2,1)}), bf16[32,8,7168]{2,1,0:T(8,128)(2,1)}, u32[]{:S(2)}, u32[]{:S(2)}) %all-to-all-start) | async-done | bytes 3670048 | tf_op jit(solution)/shard_map/all_to_all | solution.py:112
  167.8 3.3 broadcast_in_dim.12
  171.1 9.9 %all-to-all-start.2 = ((bf16[32,8,7168]{2,1,0:T(8,128)(2,1)}), bf16[32,8,7168]{2,1,0:T(8,128)(2,1)}, u32[]{:S(2)}, u32[]{:S(2)}) async-start(bf16[32,8,7168]{2,1,0:T(8,128)(2,1)} %bitcast.144), calls=%async_computation.2 | async-start | bytes 7340032 | tf_op jit(solution)/shard_map/all_to_all | solution.py:128
  181.1 4.4 %fusion.16 = f32[256,128]{1,0:T(8,128)} fusion(bf16[32,8,7168]{2,1,0:T(8,128)(2,1)} %all-to-all-done, bf16[1,1,7168,128]{3,2,1,0:T(8,128)(2,1)} %param.19), kind=kOutput, calls=%fused_computation.32 | convolution fusion | flops 469762048 | bytes 5636096 | tf_op jit(solution)/shard_map/dot_general | solution.py:42
  185.4 6.6 %fusion.2 = bf16[32,8,7168]{2,1,0:T(8,128)(2,1)} fusion(bf16[1,1,128,7168]{3,2,1,0:T(8,128)(2,1)S(1)} %copy-done, bf16[1,1,7168,128]{3,2,1,0:T(8,128)(2,1)} %param.20, bf16[32,8,7168]{2,1,0:T(8,128)(2,1)} %all-to-all-done, f32[256,128]{1,0:T(8,128)} %fusion.16), kind=kOutput, calls=%fused_computation.5 | convolution fusion | flops 941555712 | bytes 11141120 | tf_op jit(solution)/shard_map/dot_general | solution.py:45
  192.0 31.6 %all-to-all-done.2 = bf16[32,8,7168]{2,1,0:T(8,128)(2,1)} async-done(((bf16[32,8,7168]{2,1,0:T(8,128)(2,1)}), bf16[32,8,7168]{2,1,0:T(8,128)(2,1)}, u32[]{:S(2)}, u32[]{:S(2)}) %all-to-all-start.2) | async-done | bytes 3670048 | tf_op jit(solution)/shard_map/all_to_all | solution.py:128
  223.6 9.9 %all-to-all-start.1 = ((bf16[32,8,7168]{2,1,0:T(8,128)(2,1)}), bf16[32,8,7168]{2,1,0:T(8,128)(2,1)}, u32[]{:S(2)}, u32[]{:S(2)}) async-start(bf16[32,8,7168]{2,1,0:T(8,128)(2,1)} %fusion.2), calls=%async_computation.1 | async-start | bytes 7340032 | tf_op jit(solution)/shard_map/all_to_all | solution.py:114
  233.6 3.3 fusion.12
  238.4 2.9 fusion.1
  241.3 34.9 %all-to-all-done.1 = bf16[32,8,7168]{2,1,0:T(8,128)(2,1)} async-done(((bf16[32,8,7168]{2,1,0:T(8,128)(2,1)}), bf16[32,8,7168]{2,1,0:T(8,128)(2,1)}, u32[]{:S(2)}, u32[]{:S(2)}) %all-to-all-start.1) | async-done | bytes 3670048 | tf_op jit(solution)/shard_map/all_to_all | solution.py:114
  276.2 9.9 %all-to-all-start.4 = ((bf16[32,8,7168]{2,1,0:T(8,128)(2,1)}), bf16[32,8,7168]{2,1,0:T(8,128)(2,1)}, u32[]{:S(2)}, u32[]{:S(2)}) async-start(bf16[32,8,7168]{2,1,0:T(8,128)(2,1)} %fusion.1), calls=%async_computation.4 | async-start | bytes 7340032 | tf_op jit(solution)/shard_map/all_to_all | solution.py:143
  286.1 2.7 convert_reduce_fusion.2
  288.9 3.5 fusion.7
  292.4 1.9 collective-permute-start
  294.5 34.2 %all-to-all-done.4 = bf16[32,8,7168]{2,1,0:T(8,128)(2,1)} async-done(((bf16[32,8,7168]{2,1,0:T(8,128)(2,1)}), bf16[32,8,7168]{2,1,0:T(8,128)(2,1)}, u32[]{:S(2)}, u32[]{:S(2)}) %all-to-all-start.4) | async-done | bytes 3670048 | tf_op jit(solution)/shard_map/all_to_all | solution.py:143
  328.7 2.7 convert_reduce_fusion.1
  331.4 2.7 fusion.29
  335.0 5.9 %collective-permute-start.1 = (bf16[1,96,7168]{2,1,0:T(8,128)(2,1)S(1)}, bf16[1,96,7168]{2,1,0:T(8,128)(2,1)S(1)}, u32[]{:S(2)}, u32[]{:S(2)}) collective-permute-start(bf16[1,96,7168]{2,1,0:T(8,128)(2,1)S(1)} %fusion.42), channel_id=1, source_target_pairs={{0,224},{32,0},{64,32},{96,64},{128,96},{160,128},{192,160},{224,1... | collective-permute-start | bytes 4128776 | tf_op jit(solution)/shard_map/ppermute | solution.py:16
  341.6 28.1 %collective-permute-done.1 = bf16[1,96,7168]{2,1,0:T(8,128)(2,1)S(1)} collective-permute-done((bf16[1,96,7168]{2,1,0:T(8,128)(2,1)S(1)}, bf16[1,96,7168]{2,1,0:T(8,128)(2,1)S(1)}, u32[]{:S(2)}, u32[]{:S(2)}) %collective-permute-start.1) | collective-permute-done | bytes 1376288 | tf_op jit(solution)/shard_map/ppermute | solution.py:16
  369.7 2.5 copy.34
  (73 shorter events, 13.0 us)
Async XLA Ops:
  0.6 58.5 %copy-start = (bf16[1,1,128,7168]{3,2,1,0:T(8,128)(2,1)S(1)}, bf16[1,1,128,7168]{3,2,1,0:T(8,128)(2,1)}, u32[]{:S(2)}) copy-start(bf16[1,1,128,7168]{3,2,1,0:T(8,128)(2,1)} %param.21) | copy-start | bytes 5505028
  1.9 4.0 %copy-start.11 = (f32[4,96]{1,0:T(4,128)}, f32[4,96]{1,0:T(4,128)S(1)}, u32[]{:S(2)}) copy-start(f32[4,96]{1,0:T(4,128)S(1)} %copy.29) | copy-start | bytes 4612
  3.6 2.3 copy-start.19
  5.9 50.6 %copy-start.1 = (bf16[1,1,7168,128]{3,2,1,0:T(8,128)(2,1)S(1)}, bf16[1,1,7168,128]{3,2,1,0:T(8,128)(2,1)}, u32[]{:S(2)}) copy-start(bf16[1,1,7168,128]{3,2,1,0:T(8,128)(2,1)} %param.19) | copy-start | bytes 5505028
  56.5 1.5 copy-start.3
  62.1 7.2 %copy-start.13 = (f32[1,96,8]{1,2,0:T(8,128)S(1)}, f32[1,96,8]{1,2,0:T(8,128)}, u32[]{:S(2)}) copy-start(f32[1,96,8]{1,2,0:T(8,128)} %param.16) | copy-start | bytes 9220
  62.1 7.3 %copy-start.18 = (s32[1,96,8]{1,2,0:T(8,128)S(1)}, s32[1,96,8]{1,2,0:T(8,128)}, u32[]{:S(2)}) copy-start(s32[1,96,8]{1,2,0:T(8,128)} %param.14) | copy-start | bytes 9220
  62.1 13.0 %copy-start.6 = (bf16[1,96,7168]{2,1,0:T(8,128)(2,1)S(1)}, bf16[1,96,7168]{2,1,0:T(8,128)(2,1)}, u32[]{:S(2)}) copy-start(bf16[1,96,7168]{2,1,0:T(8,128)(2,1)} %param.11) | copy-start | bytes 4128772
  62.1 13.3 %copy-start.10 = (f32[1,7168]{1,0:T(1,128)S(1)}, f32[1,7168]{1,0:T(1,128)}, u32[]{:S(2)}) copy-start(f32[1,7168]{1,0:T(1,128)} %param.18) | copy-start | bytes 86020
  62.1 49.8 %all-to-all-start.5 = ((bf16[32,8,7168]{2,1,0:T(8,128)(2,1)}), bf16[32,8,7168]{2,1,0:T(8,128)(2,1)}, u32[]{:S(2)}, u32[]{:S(2)}) async-start(bf16[32,8,7168]{2,1,0:T(8,128)(2,1)} %fusion.3), calls=%async_computation.5 | async-start | bytes 7340032 | tf_op jit(solution)/shard_map/all_to_all | solution.py:144
  115.3 52.5 %all-to-all-start = ((bf16[32,8,7168]{2,1,0:T(8,128)(2,1)}), bf16[32,8,7168]{2,1,0:T(8,128)(2,1)}, u32[]{:S(2)}, u32[]{:S(2)}) async-start(bf16[32,8,7168]{2,1,0:T(8,128)(2,1)} %bitcast.143), calls=%async_computation | async-start | bytes 7340032 | tf_op jit(solution)/shard_map/all_to_all | solution.py:112
  125.2 2.8 copy-start.7
  125.2 2.8 copy-start.12
  171.1 52.5 %all-to-all-start.2 = ((bf16[32,8,7168]{2,1,0:T(8,128)(2,1)}), bf16[32,8,7168]{2,1,0:T(8,128)(2,1)}, u32[]{:S(2)}, u32[]{:S(2)}) async-start(bf16[32,8,7168]{2,1,0:T(8,128)(2,1)} %bitcast.144), calls=%async_computation.2 | async-start | bytes 7340032 | tf_op jit(solution)/shard_map/all_to_all | solution.py:128
  223.6 52.5 %all-to-all-start.1 = ((bf16[32,8,7168]{2,1,0:T(8,128)(2,1)}), bf16[32,8,7168]{2,1,0:T(8,128)(2,1)}, u32[]{:S(2)}, u32[]{:S(2)}) async-start(bf16[32,8,7168]{2,1,0:T(8,128)(2,1)} %fusion.2), calls=%async_computation.1 | async-start | bytes 7340032 | tf_op jit(solution)/shard_map/all_to_all | solution.py:114
  233.6 3.3 copy-start.2
  236.9 1.5 copy-start.4
  241.3 44.8 %copy-start.9 = (f32[1,96,8]{1,2,0:T(8,128)S(1)}, f32[1,96,8]{1,2,0:T(8,128)}, u32[]{:S(2)}) copy-start(f32[1,96,8]{1,2,0:T(8,128)} %param.17) | copy-start | bytes 9220
  276.2 52.5 %all-to-all-start.4 = ((bf16[32,8,7168]{2,1,0:T(8,128)(2,1)}), bf16[32,8,7168]{2,1,0:T(8,128)(2,1)}, u32[]{:S(2)}, u32[]{:S(2)}) async-start(bf16[32,8,7168]{2,1,0:T(8,128)(2,1)} %fusion.1), calls=%async_computation.4 | async-start | bytes 7340032 | tf_op jit(solution)/shard_map/all_to_all | solution.py:143
  286.1 2.8 copy-start.15
  286.1 2.8 copy-start.16
  286.1 2.8 copy-start.17
  288.8 5.6 %copy-start.14 = (s32[1,96,8]{1,2,0:T(8,128)S(1)}, s32[1,96,8]{1,2,0:T(8,128)}, u32[]{:S(2)}) copy-start(s32[1,96,8]{1,2,0:T(8,128)} %param.15) | copy-start | bytes 9220
  292.4 39.0 %copy-start.5 = (bf16[1,96,7168]{2,1,0:T(8,128)(2,1)S(1)}, bf16[1,96,7168]{2,1,0:T(8,128)(2,1)}, u32[]{:S(2)}) copy-start(bf16[1,96,7168]{2,1,0:T(8,128)(2,1)} %param.12) | copy-start | bytes 4128772
  292.4 49.2 %collective-permute-start = (bf16[1,96,7168]{2,1,0:T(8,128)(2,1)}, bf16[1,96,7168]{2,1,0:T(8,128)(2,1)}, u32[]{:S(2)}, u32[]{:S(2)}) collective-permute-start(bf16[1,96,7168]{2,1,0:T(8,128)(2,1)} %fusion.7), channel_id=1, source_target_pairs={{0,32},{32,64},{64,96},{96,128},{128,160},{160,192},{192,224},{224... | collective-permute-start | bytes 4128776 | tf_op jit(solution)/shard_map/ppermute | solution.py:16
  331.3 2.7 copy-start.8
  331.3 2.7 copy-start.20
  335.0 34.7 %collective-permute-start.1 = (bf16[1,96,7168]{2,1,0:T(8,128)(2,1)S(1)}, bf16[1,96,7168]{2,1,0:T(8,128)(2,1)S(1)}, u32[]{:S(2)}, u32[]{:S(2)}) collective-permute-start(bf16[1,96,7168]{2,1,0:T(8,128)(2,1)S(1)} %fusion.42), channel_id=1, source_target_pairs={{0,224},{32,0},{64,32},{96,64},{128,96},{160,128},{192,160},{224,1... | collective-permute-start | bytes 4128776 | tf_op jit(solution)/shard_map/ppermute | solution.py:16
where the time goes:
time: 377 us; the launch traced here: 373 us
  waiting for transfers between devices  202 us (54%)
  starting transfers between devices  54.7 us (15%)
  blocking collectives  50.6 us (13%)
  matrix products  34.7 us (9%)
  other arithmetic  15.6 us (4%)
  local copies, waits for them, and re-layouts  14.6 us (4%)
    all_to_all x1, blocking collectives, per_device(): lax.all_to_all(send_rows, 'expert', split_axis=0, concat_axis=0, tiled=True)  50.6 us
    all_to_all x1, waiting for transfers between devices, per_device(): lax.all_to_all(send_f, 'expert', split_axis=0, concat_axis=0, tiled=True)  38.7 us
    all_to_all x1, waiting for transfers between devices, per_device(): lax.all_to_all(outputs.reshape(received.shape), 'expert', split_axis=0, c...  34.9 us
    all_to_all x1, waiting for transfers between devices, per_device(): lax.all_to_all(second, 'expert', split_axis=0, concat_axis=0, tiled=True)  34.5 us
    all_to_all x1, waiting for transfers between devices, per_device(): lax.all_to_all(first, 'expert', split_axis=0, concat_axis=0, tiled=True)  34.2 us
    all_to_all x1, waiting for transfers between devices, per_device(): lax.all_to_all(send_cot, 'expert', split_axis=0, concat_axis=0, tiled=True)  31.6 us
    ppermute x2, waiting for transfers between devices, shifted(): lax.ppermute(array, axis, [(i, (i + by) % size) for i in range(size)])  28.1 us
    all_to_all x1, starting transfers between devices, per_device(): lax.all_to_all(send_cot, 'expert', split_axis=0, concat_axis=0, tiled=True)  9.92 us
  transfers between devices with their start and end apart: 7, of which 6 were waited for; matrix products, arithmetic and copies ran while one was open for 12% of the time, Pallas kernels for 0%

commit v1 on v0

v1 whole, which is shorter than its diff:
```python
import functools

import jax
import jax.numpy as jnp
from jax import lax
from jax.experimental import pallas as pl
from jax.experimental.pallas import tpu as pltpu
from jax.sharding import PartitionSpec as P

GROUP = 8
CAP = 8
CORES = 2
LANES = 128
EPSILON = 1e-06
ROUTE_SCALE = 2.5
VMEM_LIMIT = 24 * 1024 * 1024

bf16 = jnp.bfloat16
f32 = jnp.float32


def params():
    return pltpu.CompilerParams(vmem_limit_bytes=VMEM_LIMIT)


def cost(flops, bytes_accessed):
    return pl.CostEstimate(flops=flops, bytes_accessed=bytes_accessed, transcendentals=0)


def dot(a, b, dims=((1,), (0,)), precision=None):
    return lax.dot_general(a, b, (dims, ((), ())), precision=precision, preferred_element_type=f32)


def exact(a, b, dims=((1,), (0,))):
    return dot(a, b, dims, lax.Precision.HIGHEST)


def sigmoid(v):
    return 1.0 / (1.0 + jnp.exp(-v))


def after(array, *others):
    return lax.optimization_barrier((array,) + others)[0]


def split_dot(weights, rows):
    high = weights.astype(bf16)
    low = (weights - high.astype(f32)).astype(bf16)
    return dot(high, rows) + dot(low, rows)


def slot_expert(slots, rows):
    return lax.broadcasted_iota(jnp.int32, (slots, rows), 0) // CAP


def gate_values(scores):
    affinity = sigmoid(scores)
    total = jnp.sum(affinity, axis=0, keepdims=True)
    return affinity, total, ROUTE_SCALE * affinity / total


def tables(routes, scores, slots):
    topk, rows = routes.shape
    expert = slot_expert(slots, rows)
    _, _, gates = gate_values(scores)
    naming = jnp.zeros((slots, rows), f32)
    weight = jnp.zeros((slots, rows), f32)
    for j in range(topk):
        hit = routes[j : j + 1, :] == expert
        naming = naming + jnp.where(hit, 1.0, 0.0)
        weight = weight + jnp.where(hit, gates[j : j + 1, :], 0.0)
    shape = (rows, rows)
    above = lax.broadcasted_iota(jnp.int32, shape, 0) < lax.broadcasted_iota(jnp.int32, shape, 1)
    earlier = dot(naming.astype(bf16), jnp.where(above, 1.0, 0.0).astype(bf16))
    slot = lax.rem(lax.broadcasted_iota(jnp.int32, (slots, rows), 0), CAP)
    here = earlier == slot.astype(f32)
    table = jnp.where(here, naming, 0.0)
    mixing = jnp.where(here, weight, 0.0)
    shape = (slots, slots)
    to = lax.broadcasted_iota(jnp.int32, shape, 0)
    from_ = lax.broadcasted_iota(jnp.int32, shape, 1)
    lower = (lax.rem(from_, CAP) == 0) & (from_ // CAP < to // CAP)
    before = dot(jnp.where(lower, 1.0, 0.0).astype(bf16), naming.astype(bf16))
    first = jnp.where(before == 0.0, table, 0.0)
    return table, mixing, first


def prep_bwd_kernel(
    steps, routes_ref, scores_ref, x_ref, cot_ref, gain_ref, cb_ref, xs_ref, cs_ref, first_ref,
    table_ref, weights_ref, inverse_ref, take_ref, x_slots_ref, c_slots_ref
):
    step = pl.program_id(0)
    slots = take_ref.shape[0]
    block = x_ref.shape[1]

    @pl.when(step == 0)
    def _():
        table, mixing, first = tables(routes_ref[...], scores_ref[...], slots)
        first_ref[...] = first
        table_ref[...] = table
        weights_ref[...] = exact(table, mixing, ((1,), (1,)))
        take_ref[...] = table.astype(bf16)

    take = take_ref[...]
    lanes = pl.ds(pl.multiple_of(step * block, LANES), block)
    x_slots_ref[:, lanes] = dot(take, x_ref[...])
    c_slots_ref[:, lanes] = dot(take, cot_ref[...])

    @pl.when(step == steps - 1)
    def _():
        x = x_slots_ref[...]
        c = c_slots_ref[...]
        inverse = lax.rsqrt(jnp.mean(x * x, axis=1, keepdims=True) + EPSILON)
        inverse_ref[...] = jnp.broadcast_to(inverse, inverse_ref.shape)
        normed = x * inverse * gain_ref[...]
        xs_ref[...] = x.astype(bf16)
        cs_ref[...] = c.astype(bf16)
        for k in range(slots // CAP):
            part = slice(k * CAP, (k + 1) * CAP)
            both = jnp.concatenate([c[part], normed[part]], axis=0).astype(bf16)
            cb_ref[2 * k * CAP : 2 * (k + 1) * CAP, :] = both


def prep_fwd_kernel(
    steps, routes_ref, scores_ref, x_ref, gain_ref, out_ref, mixing_ref, take_ref,
    x_slots_ref
):
    step = pl.program_id(0)
    slots = take_ref.shape[0]
    block = x_ref.shape[1]

    @pl.when(step == 0)
    def _():
        table, mixing, _ = tables(routes_ref[...], scores_ref[...], slots)
        mixing_ref[...] = mixing
        take_ref[...] = table.astype(bf16)

    lanes = pl.ds(pl.multiple_of(step * block, LANES), block)
    x_slots_ref[:, lanes] = dot(take_ref[...], x_ref[...])

    @pl.when(step == steps - 1)
    def _():
        x = x_slots_ref[...]
        inverse = lax.rsqrt(jnp.mean(x * x, axis=1, keepdims=True) + EPSILON)
        out_ref[...] = (x * inverse * gain_ref[...]).astype(bf16)


def vmem():
    return pl.BlockSpec(memory_space=pltpu.VMEM)


def whole(shape):
    return pl.BlockSpec(shape, lambda *_: (0,) * len(shape))


def across(rows, block):
    return pl.BlockSpec((rows, block), lambda i: (0, i))


def prep_bwd(routes, scores, x, cot, gain, window):
    rows, width = x.shape
    slots = window * CAP
    steps = 4
    block = width // steps
    shapes = [
        ((2 * slots, width), bf16),
        ((slots, width), bf16),
        ((slots, width), bf16),
        ((slots, rows), f32),
        ((slots, rows), f32),
        ((slots, slots), f32),
        ((slots, LANES), f32),
    ]
    return pl.pallas_call(
        functools.partial(prep_bwd_kernel, steps),
        out_shape=[jax.ShapeDtypeStruct(*s) for s in shapes],
        grid=(steps,),
        in_specs=[whole(routes.shape), whole(scores.shape)]
        + [across(rows, block)] * 2
        + [whole(gain.shape)],
        out_specs=[whole(s[0]) for s in shapes],
        scratch_shapes=[
            pltpu.VMEM((slots, rows), bf16),
            pltpu.VMEM((slots, width), f32),
            pltpu.VMEM((slots, width), f32),
        ],
        compiler_params=params(),
        cost_estimate=cost(4 * slots * rows * width, 8 * rows * width),
        name="prep_bwd",
    )(routes, scores, x, cot, gain)


def prep_fwd(routes, scores, x, gain, window):
    rows, width = x.shape
    slots = window * CAP
    steps = 4
    block = width // steps
    return pl.pallas_call(
        functools.partial(prep_fwd_kernel, steps),
        out_shape=[
            jax.ShapeDtypeStruct((slots, width), bf16),
            jax.ShapeDtypeStruct((slots, rows), f32),
        ],
        grid=(steps,),
        in_specs=[whole(routes.shape), whole(scores.shape)]
        + [across(rows, block), whole(gain.shape)],
        out_specs=[whole((slots, width)), whole((slots, rows))],
        scratch_shapes=[pltpu.VMEM((slots, rows), bf16), pltpu.VMEM((slots, width), f32)],
        compiler_params=params(),
        cost_estimate=cost(2 * slots * rows * width, 4 * rows * width),
        name="prep_fwd",
    )(routes, scores, x, gain)


def enter_bwd_kernel(steps, chunks, *refs):
    cot_refs, row_refs = refs[:chunks], refs[chunks : 2 * chunks]
    gate_ref, up_ref, down_ref, both_ref, dh_ref = refs[2 * chunks :]
    step = pl.program_id(0)
    weights = jnp.concatenate([gate_ref[...], up_ref[...]], axis=1)
    both = dot(jnp.concatenate([r[...] for r in row_refs], axis=0), weights)
    cots = jnp.concatenate([r[...] for r in cot_refs], axis=0)
    dh = dot(cots, down_ref[...], ((1,), (1,)))

    @pl.when(step == 0)
    def _():
        both_ref[...] = both
        dh_ref[...] = dh

    @pl.when(step > 0)
    def _():
        both_ref[...] += both
        dh_ref[...] += dh


def enter_bwd(cots, inputs, gate, up, down):
    width, hidden = gate.shape
    steps = 4
    block = width // steps
    part = 32
    total = len(cots) * part
    pick = lambda k: pl.BlockSpec((part, block), lambda i: (k, i))
    return pl.pallas_call(
        functools.partial(enter_bwd_kernel, steps, len(cots)),
        out_shape=[
            jax.ShapeDtypeStruct((total, 2 * hidden), f32),
            jax.ShapeDtypeStruct((total, hidden), f32),
        ],
        grid=(steps,),
        in_specs=[pick(k) for _, k in cots + inputs]
        + [pl.BlockSpec((block, hidden), lambda i: (i, 0))] * 2
        + [pl.BlockSpec((hidden, block), lambda i: (0, i))],
        out_specs=[whole((total, 2 * hidden)), whole((total, hidden))],
        compiler_params=params(),
        cost_estimate=cost(6 * total * width * hidden, 4 * total * width + 6 * width * hidden),
        name="enter_bwd",
    )(*[a for a, _ in cots + inputs], gate, up, down)


def leave_bwd_kernel(steps, near_both, near_dh, far_both, far_dh, gate_ref, up_ref, *refs):
    own_ref, peer_ref, da_ref, q_ref = refs
    step = pl.program_id(0)
    hidden = gate_ref.shape[1]
    block = gate_ref.shape[0]

    @pl.when(step == 0)
    def _():
        n, m = near_dh.shape[0] // 2, far_dh.shape[0] // 2

        def joined(a, b):
            return jnp.concatenate([a[:n], b[:m], a[n:], b[m:]], axis=0)

        both = joined(near_both[...], far_both[...])
        dh = joined(near_dh[...], far_dh[...])
        pre_gate = both[:, :hidden]
        pre_up = both[:, hidden:]
        sig = sigmoid(pre_gate)
        active = pre_gate * sig
        h = (active * pre_up).astype(bf16).astype(f32)
        da = dh * pre_up * sig * (1.0 + pre_gate * (1.0 - sig))
        db = dh * active
        da_ref[...] = jnp.concatenate([da, db], axis=1).astype(bf16)
        q = jnp.sum(dh * h, axis=1, keepdims=True)
        q_ref[...] = jnp.broadcast_to(q, q_ref.shape).astype(bf16)

    weights = jnp.concatenate([gate_ref[...], up_ref[...]], axis=1)
    grads = dot(da_ref[...], weights, ((1,), (1,))).astype(bf16)
    lanes = pl.ds(pl.multiple_of(step * block, LANES), block)
    middle = grads.shape[0] // 2
    own_ref[:, lanes] = grads[:middle]
    peer_ref[:, lanes] = grads[middle:]

    @pl.when(step == steps - 1)
    def _():
        own_ref[:, steps * block :] = q_ref[:middle, :]
        peer_ref[:, steps * block :] = q_ref[middle:, :]


def leave_bwd(near, far, gate, up):
    width, hidden = gate.shape
    steps = 4
    block = width // steps
    total = near[1].shape[0] + far[1].shape[0]
    out = jax.ShapeDtypeStruct((total // 2, width + LANES), bf16)
    small = [*near, *far]
    return pl.pallas_call(
        functools.partial(leave_bwd_kernel, steps),
        out_shape=[out, out],
        grid=(steps,),
        in_specs=[whole(a.shape) for a in small]
        + [pl.BlockSpec((block, hidden), lambda i: (i, 0))] * 2,
        out_specs=[whole(out.shape)] * 2,
        scratch_shapes=[pltpu.VMEM((total, 2 * hidden), bf16), pltpu.VMEM((total, LANES), bf16)],
        compiler_params=params(),
        cost_estimate=cost(4 * total * width * hidden, 2 * total * width + 4 * width * hidden),
        name="leave_bwd",
    )(*small, gate, up)


def expert_fwd_kernel(steps, chunks, *refs):
    rows_refs = refs[:chunks]
    gate_ref, up_ref, down_ref, own_ref, peer_ref, both_ref, h_ref = refs[chunks:]
    step = pl.program_id(0)
    hidden = gate_ref.shape[1]
    block = gate_ref.shape[0]

    @pl.when(step < steps)
    def _():
        weights = jnp.concatenate([gate_ref[...], up_ref[...]], axis=1)
        both = dot(jnp.concatenate([r[...] for r in rows_refs], axis=0), weights)

        @pl.when(step == 0)
        def _():
            both_ref[...] = both

        @pl.when(step > 0)
        def _():
            both_ref[...] += both

    @pl.when(step == steps - 1)
    def _():
        pre_gate = both_ref[:, :hidden]
        h_ref[...] = (pre_gate * sigmoid(pre_gate) * both_ref[:, hidden:]).astype(bf16)

    @pl.when(step >= steps)
    def _():
        outs = dot(h_ref[...], down_ref[...]).astype(bf16)
        lanes = pl.ds(pl.multiple_of((step - steps) * block, LANES), block)
        middle = outs.shape[0] // 2
        own_ref[:, lanes] = outs[:middle]
        peer_ref[:, lanes] = outs[middle:]


def expert_fwd(own, peer, gate, up, down):
    width, hidden = gate.shape
    steps = 4
    block = width // steps
    chunks = own + peer
    rows = sum(c.shape[0] for c in own)
    take = lambda i: jnp.minimum(i, steps - 1)
    out = jax.ShapeDtypeStruct((rows, width), bf16)
    return pl.pallas_call(
        functools.partial(expert_fwd_kernel, steps, len(chunks)),
        out_shape=[out, out],
        grid=(2 * steps,),
        in_specs=[pl.BlockSpec((c.shape[0], block), lambda i: (0, take(i))) for c in chunks]
        + [
            pl.BlockSpec((block, hidden), lambda i: (take(i), 0)),
            pl.BlockSpec((block, hidden), lambda i: (take(i), 0)),
            pl.BlockSpec((hidden, block), lambda i: (0, jnp.maximum(i - steps, 0))),
        ],
        out_specs=[whole(out.shape)] * 2,
        scratch_shapes=[
            pltpu.VMEM((2 * rows, 2 * hidden), f32),
            pltpu.VMEM((2 * rows, hidden), bf16),
        ],
        compiler_params=params(),
        cost_estimate=cost(12 * rows * width * hidden, 8 * rows * width + 6 * width * hidden),
        name="expert_fwd",
    )(*chunks, gate, up, down)


def grad_slots_kernel(
    routes_ref, scores_ref, table_ref, weights_ref, inverse_ref, xs_ref, cs_ref, gain_ref, dn_ref,
    grad_ref, score_ref
):
    slots, width = xs_ref.shape
    t = split_dot(weights_ref[...], dn_ref[:, :width]) * gain_ref[...]
    x = xs_ref[...].astype(f32)
    inverse = inverse_ref[:, :1]
    mean = jnp.mean(x * t, axis=1, keepdims=True)
    grad = cs_ref[...].astype(f32) + inverse * t - x * (inverse * inverse * inverse * mean)
    grad_ref[...] = grad.astype(bf16)

    routes = routes_ref[...]
    topk, rows = routes.shape
    spread = table_ref[...] * dn_ref[:, width:].astype(f32)[:, :1]
    expert = slot_expert(slots, rows)
    place = lax.broadcasted_iota(jnp.int32, (topk, rows), 0)
    dgate = jnp.zeros((topk, rows), f32)
    for j in range(topk):
        hit = routes[j : j + 1, :] == expert
        value = jnp.sum(jnp.where(hit, spread, 0.0), axis=0, keepdims=True)
        dgate = jnp.where(place == j, value, dgate)
    affinity, total, gates = gate_values(scores_ref[...])
    term = jnp.sum(dgate * gates, axis=0, keepdims=True) / ROUTE_SCALE
    score_ref[...] = affinity * (1.0 - affinity) * (ROUTE_SCALE / total) * (dgate - term)


def grad_slots(routes, scores, table, weights, inverse, xs, cs, gain, dn):
    slots, width = xs.shape
    return pl.pallas_call(
        grad_slots_kernel,
        out_shape=[
            jax.ShapeDtypeStruct((slots, width), bf16),
            jax.ShapeDtypeStruct(scores.shape, f32),
        ],
        in_specs=[vmem()] * 9,
        out_specs=[vmem()] * 2,
        compiler_params=params(),
        cost_estimate=cost(4 * slots * slots * width, 8 * slots * width),
        name="grad_slots",
    )(routes, scores, table, weights, inverse, xs, cs, gain, dn)


def stacked(refs):
    return jnp.concatenate([r[...].astype(f32) for r in refs], axis=0)


def place_grad_kernel(first_ref, top_ref, bottom_ref, slots_ref, out_ref):
    first = first_ref[...].astype(bf16)
    touched = dot(first, jnp.ones((first.shape[0], LANES), bf16), ((0,), (0,)))[:, :1]
    placed = dot(first, slots_ref[...], ((0,), (0,)))
    out_ref[...] = jnp.where(touched > 0.0, placed, stacked([top_ref, bottom_ref])).astype(bf16)


def place_fwd_kernel(mixing_ref, top_ref, bottom_ref, *refs):
    out_ref = refs[-1]
    mixing = mixing_ref[...]
    high = mixing.astype(bf16)
    low = (mixing - high.astype(f32)).astype(bf16)
    rows = stacked(refs[:-1]).astype(bf16)
    branch = dot(high, rows, ((0,), (0,))) + dot(low, rows, ((0,), (0,)))
    out_ref[...] = (stacked([top_ref, bottom_ref]) + branch).astype(bf16)


def place(kernel, name, table, early, *blocks):
    slots, rows = table.shape
    width = early[0].shape[1]
    steps = 4
    block = width // steps
    return pl.pallas_call(
        kernel,
        out_shape=jax.ShapeDtypeStruct((rows, width), bf16),
        grid=(steps,),
        in_specs=[whole(table.shape)] + [across(b.shape[0], block) for b in [*early, *blocks]],
        out_specs=across(rows, block),
        compiler_params=params(),
        cost_estimate=cost(4 * rows * slots * width, 6 * rows * width),
        name=name,
    )(table, *early, *blocks)


class Net:
    def __init__(self, sections, devices, window):
        self.sections, self.devices = sections, devices
        self.rows = window
        self.columns = devices // window // CORES
        self.row_groups = [
            [self.index(y, x, c) for y in range(self.rows)]
            for x in range(self.columns)
            for c in range(CORES)
        ]

    def index(self, y, x, c):
        return ((y % self.rows) * self.columns + x % self.columns) * CORES + c % CORES

    def pairs(self, dy, dx, dc):
        return [
            (self.index(y, x, c), self.index(y + dy, x + dx, c + dc))
            for y in range(self.rows)
            for x in range(self.columns)
            for c in range(CORES)
        ]

    def move(self, array, dy=0, dx=0, dc=0):
        return lax.ppermute(array, "expert", self.pairs(dy, dx, dc))

    def relay(self, array, by, dy=0):
        if dy == 0:
            pairs = [(s, (s + by) % self.sections) for s in range(self.sections)]
            return lax.ppermute(array, "section", pairs)
        pairs = [
            (s * self.devices + i, ((s + by) % self.sections) * self.devices + j)
            for s in range(self.sections)
            for i, j in self.pairs(dy, 0, 0)
        ]
        return lax.ppermute(array, ("section", "expert"), pairs)

    def exchange(self, array):
        blocks = array.reshape(self.rows, -1, array.shape[-1])
        out = lax.all_to_all(
            blocks, "expert", 0, 0, tiled=True, axis_index_groups=self.row_groups
        )
        return out.reshape(array.shape)

    def near(self, mine):
        return self.move(mine, dx=1), self.move(mine, dx=-1)

    def far(self, left, right):
        middle = left.shape[0] // 2
        return self.move(left[:middle], dx=1), self.move(right[middle:], dx=-1)

    def swap(self, arrays):
        return [self.move(a, dc=1) for a in arrays]

    def collect(self, own, other):
        total = own.astype(f32) + other.astype(f32)
        rows = own.shape[0] // 4
        mine, left, right, far = [total[i * rows : (i + 1) * rows] for i in range(4)]
        middle = rows // 2
        far = far.astype(bf16)
        to_right = self.move(far[:middle], dx=1).astype(f32)
        to_left = self.move(far[middle:], dx=-1).astype(f32)
        right = jnp.concatenate([right[:middle] + to_right, right[middle:]], axis=0)
        left = jnp.concatenate([left[:middle], left[middle:] + to_left], axis=0)
        from_left = self.move(right.astype(bf16), dx=1).astype(f32)
        from_right = self.move(left.astype(bf16), dx=-1).astype(f32)
        return (mine + from_left + from_right).astype(bf16)


def block_of(array, index, rows, count=1):
    return lax.dynamic_slice_in_dim(array, index * rows, rows * count, axis=0)


def per_device(
    fwd_input,
    saved_input,
    out_cotangent,
    fwd_routes,
    bwd_routes,
    fwd_scores,
    bwd_scores,
    norm_gain,
    gate_proj,
    up_proj,
    down_proj,
):
    devices = lax.axis_size("expert")
    window = devices // GROUP
    net = Net(lax.axis_size("section"), devices, window)
    gate, up, down = gate_proj[0, 0], up_proj[0, 0], down_proj[0, 0]
    gain = norm_gain
    x_f, x_b, cot = fwd_input[0], saved_input[0], out_cotangent[0]
    routes_f, routes_b = fwd_routes[0].T, bwd_routes[0].T
    scores_f, scores_b = fwd_scores[0].T, bwd_scores[0].T
    width = x_f.shape[1]
    middle = x_f.shape[0] // 2
    row = lax.axis_index("expert") // GROUP
    cb, xs, cs, first, table, weights, inverse = prep_bwd(
        routes_b, scores_b, x_b, cot, gain, window
    )
    rows_f, mixing = prep_fwd(routes_f, scores_f, x_f, gain, window)

    mine_b = net.exchange(cb).reshape(window, 2, CAP, width)
    mine_b = mine_b.transpose(1, 0, 2, 3).reshape(cb.shape)
    top_f = net.relay(x_f[:middle], 1)
    top_c = net.relay(cot[:middle], -1)
    mixing = block_of(jnp.concatenate([mixing, mixing], axis=0), row, CAP, window)
    mixing = net.relay(mixing, 1)
    first = net.relay(first, -1)
    mine_b, rows_f, top_f, top_c, mixing, first = lax.optimization_barrier(
        (mine_b, rows_f, top_f, top_c, mixing, first)
    )

    left_b, right_b = net.near(mine_b)
    mine_f = net.exchange(rows_f)
    bottom_f = net.relay(after(x_f, rows_f)[middle:], 1)
    bottom_c = net.relay(after(cot, rows_f)[middle:], -1)
    left_b, right_b, mine_f, bottom_f, bottom_c = lax.optimization_barrier(
        (left_b, right_b, mine_f, bottom_f, bottom_c)
    )

    far_b = net.far(left_b, right_b)
    near_f = net.near(mine_f)
    near_b = [mine_b, left_b, right_b]
    near_b = near_b + net.swap(near_b)
    near_h = enter_bwd([(a, 0) for a in near_b], [(a, 1) for a in near_b], gate, up, down)
    far_b, near_f, near_h = lax.optimization_barrier((far_b, near_f, near_h))

    far_f = net.far(*near_f)
    own_f = [mine_f, *near_f, *far_f]
    far_b = [*far_b, *net.swap(far_b)]
    far_h = enter_bwd([(a, 0) for a in far_b[0::2]], [(a, 0) for a in far_b[1::2]], gate, up, down)
    own, peer = leave_bwd(near_h, far_h, gate, up)
    other = net.move(peer, dc=1)
    peer_f = net.swap(own_f)
    own, other, own_f, peer_f = lax.optimization_barrier((own, other, own_f, peer_f))

    dn = net.exchange(net.collect(own, other))
    own, peer = expert_fwd(own_f, peer_f, gate, up, down)
    outs = net.collect(own, net.move(peer, dc=1))
    outs = [
        net.relay(block_of(outs, lax.rem(row + window - d, window), CAP), 1, dy=-d)
        for d in range(window)
    ]
    grads, score_rows = grad_slots(
        routes_b, scores_b, table, weights, inverse, xs, cs, gain, dn
    )
    late_b = net.relay(grads, -1)
    fwd_handoff = place(place_fwd_kernel, "place_fwd", mixing, (top_f, bottom_f), *outs)
    grad_handoff = place(place_grad_kernel, "place_grad", first, (top_c, bottom_c), late_b)
    return (fwd_handoff[None], grad_handoff[None], score_rows.T[None])


def solution(mesh):
    tokens = P("section", "expert", None)
    slices = P("section", "expert", None, None)
    in_specs = (tokens,) * 7 + (P("section", None),) + (slices,) * 3
    return jax.shard_map(
        per_device, mesh=mesh, in_specs=in_specs, out_specs=(tokens,) * 3, check_vma=False
    )
```

time: 377 us -> 178 us (0.47)
  waiting for transfers between devices: 202 us -> 71.4 us
  blocking collectives: 50.6 us -> 0 us
  matrix products: 34.7 us -> 0 us
  Pallas kernels: 0 us -> 25.4 us
  other arithmetic: 15.6 us -> 3.59 us
  local copies, waits for them, and re-layouts: 14.6 us -> 18.8 us
    all_to_all x5 -> x3, waiting for transfers between devices: 174 us -> 16.2 us  [exchange(): lax.all_to_all(blocks, 'expert', 0, 0, tiled=True, axis_index_groups=self...]
    all_to_all x1 -> x0, blocking collectives: 50.6 us -> none  [per_device(): lax.all_to_all(send_rows, 'expert', split_axis=0, concat_axis=0, tiled=True)]
    ppermute x2 -> x39, starting transfers between devices: 7.85 us -> 43.8 us  [the longest x28 21.3 us: move(): return lax.ppermute(array, 'expert', self.pairs(dy, dx, dc))]
    dot_general x14 -> x0, matrix products: 34.7 us -> none  [the longest x1 6.58 us: slice_forward(): jnp.dot(hidden, w_down, preferred_element_type=jnp.float32)]
    all_to_all x5 -> x3, starting transfers between devices: 46.9 us -> 13.2 us  [exchange(): lax.all_to_all(blocks, 'expert', 0, 0, tiled=True, axis_index_groups=self...]
    ppermute x2 -> x39, waiting for transfers between devices: 28.1 us -> 55.2 us  [the longest x28 43.7 us: move(): return lax.ppermute(array, 'expert', self.pairs(dy, dx, dc))]
    pallas_call x0 -> x9, Pallas kernels: none -> 25.4 us  [the longest x2 8.22 us: place(): pl.pallas_call(kernel, out_shape=jax.ShapeDtypeStruct((rows, width), bf16...]
    reduce_sum x11 -> x0, other arithmetic: 11.8 us -> none  [the longest x1 2.77 us: per_device(): jnp.sum(second.reshape((window, group_size, capacity) + second.shape[2:])...]
  transfers between devices with their start and end apart: 7 -> 42, of which waited for: 6 -> 24; matrix products, arithmetic and copies ran while one was open for 12% -> 6% of each run, Pallas kernels for 0% -> 9%
where the time goes in v1:
time: 178 us; the launch traced here: 177 us
  waiting for transfers between devices  71.4 us (40%)
  starting transfers between devices  57 us (32%)
  Pallas kernels  25.4 us (14%)
  local copies, waits for them, and re-layouts  18.8 us (11%)
  other arithmetic  3.59 us (2%)
    ppermute x28, waiting for transfers between devices, move(): return lax.ppermute(array, 'expert', self.pairs(dy, dx, dc))  43.7 us
    ppermute x28, starting transfers between devices, move(): return lax.ppermute(array, 'expert', self.pairs(dy, dx, dc))  21.3 us
    ppermute x8, starting transfers between devices, relay(): return lax.ppermute(array, 'section', pairs)  16.5 us
    all_to_all x3, waiting for transfers between devices, exchange(): lax.all_to_all(blocks, 'expert', 0, 0, tiled=True, axis_index_groups=self...  16.2 us
    all_to_all x3, starting transfers between devices, exchange(): lax.all_to_all(blocks, 'expert', 0, 0, tiled=True, axis_index_groups=self...  13.2 us
    unnamed x50, local copies, waits for them, and re-layouts  10.4 us
    ppermute x8, waiting for transfers between devices, relay(): return lax.ppermute(array, 'section', pairs)  8.92 us
    pallas_call x2, Pallas kernels, place(): pl.pallas_call(kernel, out_shape=jax.ShapeDtypeStruct((rows, width), bf16...  8.22 us
  transfers between devices with their start and end apart: 42, of which 24 were waited for; matrix products, arithmetic and copies ran while one was open for 6% of the time, Pallas kernels for 9%

profile of v1, /device:TPU:6, one launch (start us, length us, event | category | flops | bytes accessed | tf_op | source)
XLA Modules:
  0.0 177.1 jit_solution(12620581818739772464)
XLA Ops:
  9.8 4.6 %all-to-all-start = ((bf16[4,16,7168]{2,1,0:T(8,128)(2,1)}), bf16[4,16,7168]{2,1,0:T(8,128)(2,1)}, u32[]{:S(2)}, u32[]{:S(2)}) async-start(bf16[4,16,7168]{2,1,0:T(8,128)(2,1)} %bitcast.63), calls=%async_computation | async-start | bytes 1835008 | tf_op jit(solution)/shard_map/all_to_all | solution.py:501
  18.1 3.9 %collective-permute-start.1 = (bf16[48,7168]{1,0:T(8,128)(2,1)}, bf16[48,7168]{1,0:T(8,128)(2,1)S(1)}, u32[]{:S(2)}, u32[]{:S(2)}) collective-permute-start(bf16[48,7168]{1,0:T(8,128)(2,1)} %slice_bitcast_fusion), channel_id=1, source_target_pairs={{0,224},{32,0},{64,32},{96,64},{128,96},{160,128},{192,160},{224,1... | collective-permute-start | bytes 2064392 | tf_op jit(solution)/shard_map/ppermute | solution.py:491
  24.3 3.2 %collective-permute-start.3 = (f32[32,96]{1,0:T(8,128)S(1)}, f32[32,96]{1,0:T(8,128)S(1)}, u32[]{:S(2)}, u32[]{:S(2)}) collective-permute-start(f32[32,96]{1,0:T(8,128)S(1)} %get-tuple-element.56), channel_id=1, source_target_pairs={{0,224},{32,0},{64,32},{96,64},{128,96},{160,128},{192,160},{224,1... | collective-permute-start | bytes 36872 | tf_op jit(solution)/shard_map/ppermute | solution.py:491
  29.5 7.5 %collective-permute-done.2.mixing_ref = f32[32,96]{1,0:T(8,128)S(1)} collective-permute-done((f32[32,96]{1,0:T(8,128)S(1)}, f32[32,96]{1,0:T(8,128)S(1)}, u32[]{:S(2)}, u32[]{:S(2)}) %collective-permute-start.2) | collective-permute-done | bytes 12320 | tf_op jit(solution)/shard_map/ppermute | solution.py:491
  41.2 2.2 %slice.101 = bf16[48,7168]{1,0:T(8,128)(2,1)} slice(bf16[96,7168]{1,0:T(8,128)(2,1)} %bitcast.55), slice={[48:96], [0:7168]} | slice | bytes 1376256 | tf_op jit(solution)/shard_map/slice | solution.py:578
  43.4 3.3 %collective-permute-start.7 = (bf16[48,7168]{1,0:T(8,128)(2,1)}, bf16[48,7168]{1,0:T(8,128)(2,1)}, u32[]{:S(2)}, u32[]{:S(2)}) collective-permute-start(bf16[48,7168]{1,0:T(8,128)(2,1)} %slice.101), channel_id=1, source_target_pairs={{0,224},{32,0},{64,32},{96,64},{128,96},{160,128},{192,160},{224,1... | collective-permute-start | bytes 2064392 | tf_op jit(solution)/shard_map/ppermute | solution.py:491
  46.7 4.5 %all-to-all-start.1 = ((bf16[4,8,7168]{2,1,0:T(8,128)(2,1)}), bf16[4,8,7168]{2,1,0:T(8,128)(2,1)S(1)}, u32[]{:S(2)}, u32[]{:S(2)}) async-start(bf16[4,8,7168]{2,1,0:T(8,128)(2,1)} %bitcast.64), calls=%async_computation.1 | async-start | bytes 917504 | tf_op jit(solution)/shard_map/all_to_all | solution.py:501
  51.2 7.7 %all-to-all-done.1 = bf16[4,8,7168]{2,1,0:T(8,128)(2,1)S(1)} async-done(((bf16[4,8,7168]{2,1,0:T(8,128)(2,1)}), bf16[4,8,7168]{2,1,0:T(8,128)(2,1)S(1)}, u32[]{:S(2)}, u32[]{:S(2)}) %all-to-all-start.1) | async-done | bytes 458784 | tf_op jit(solution)/shard_map/all_to_all | solution.py:501
  65.4 2.4 %collective-permute-start.10 = (bf16[32,7168]{1,0:T(8,128)(2,1)S(1)}, bf16[32,7168]{1,0:T(8,128)(2,1)S(1)}, u32[]{:S(2)}, u32[]{:S(2)}) collective-permute-start(bf16[32,7168]{1,0:T(8,128)(2,1)S(1)} %bitcast.58), channel_id=1, source_target_pairs={{0,2},{1,3},{2,4},{3,5},{4,6},{5,7},{6,0},{7,1},{8,10},{9,11},{10,... | collective-permute-start | bytes 1376264 | tf_op jit(solution)/shard_map/ppermute | solution.py:486
  69.3 4.2 %enter_bwd.2 = (f32[192,256]{1,0:T(8,128)S(1)}, f32[192,128]{1,0:T(8,128)S(1)}) custom-call(bf16[64,7168]{1,0:T(8,128)(2,1)S(1)} %bitcast.51, bf16[64,7168]{1,0:T(8,128)(2,1)} %collective-permute-done.4.refs_1_.refs_7_, bf16[64,7168]{1,0:T(8,128)(2,1)} %collective-permute-done.5.refs_2_.refs_8_, bf16[64,7168]{1,0:T(8,128)(2,1)} %collective-permute-done.12.refs_3_.refs_9_, ...), custom_call_target="tpu_custom_call" | custom-call | flops 1056964608 | bytes 11010048 | tf_op jit(solution)/shard_map/enter_bwd/pallas_call | solution.py:242
  73.6 3.2 %collective-permute-done.8.refs_0_ = bf16[32,7168]{1,0:T(8,128)(2,1)S(1)} collective-permute-done((bf16[32,7168]{1,0:T(8,128)(2,1)S(1)}, bf16[32,7168]{1,0:T(8,128)(2,1)S(1)}, u32[]{:S(2)}, u32[]{:S(2)}) %collective-permute-start.8) | collective-permute-done | bytes 458784 | tf_op jit(solution)/shard_map/ppermute | solution.py:486
  76.8 2.4 %collective-permute-done.9.refs_2_ = bf16[32,7168]{1,0:T(8,128)(2,1)S(1)} collective-permute-done((bf16[32,7168]{1,0:T(8,128)(2,1)S(1)}, bf16[32,7168]{1,0:T(8,128)(2,1)S(1)}, u32[]{:S(2)}, u32[]{:S(2)}) %collective-permute-start.9) | collective-permute-done | bytes 458784 | tf_op jit(solution)/shard_map/ppermute | solution.py:486
  79.2 6.5 %collective-permute-done.10.refs_1_ = bf16[32,7168]{1,0:T(8,128)(2,1)S(1)} collective-permute-done((bf16[32,7168]{1,0:T(8,128)(2,1)S(1)}, bf16[32,7168]{1,0:T(8,128)(2,1)S(1)}, u32[]{:S(2)}, u32[]{:S(2)}) %collective-permute-start.10) | collective-permute-done | bytes 458784 | tf_op jit(solution)/shard_map/ppermute | solution.py:486
  85.7 2.2 %collective-permute-done.11.refs_2_ = bf16[32,7168]{1,0:T(8,128)(2,1)S(1)} collective-permute-done((bf16[32,7168]{1,0:T(8,128)(2,1)S(1)}, bf16[32,7168]{1,0:T(8,128)(2,1)S(1)}, u32[]{:S(2)}, u32[]{:S(2)}) %collective-permute-start.11) | collective-permute-done | bytes 458784 | tf_op jit(solution)/shard_map/ppermute | solution.py:486
  90.3 2.1 %enter_bwd.3 = (f32[64,256]{1,0:T(8,128)S(1)}, f32[64,128]{1,0:T(8,128)S(1)}) custom-call(bf16[32,7168]{1,0:T(8,128)(2,1)S(1)} %collective-permute-done.8.refs_0_, bf16[32,7168]{1,0:T(8,128)(2,1)S(1)} %collective-permute-done.15.refs_1_, bf16[32,7168]{1,0:T(8,128)(2,1)S(1)} %collective-permute-done.9.refs_2_, ...), custom_call_target="tpu_custom_call" | custom-call | flops 352321536 | bytes 7340032 | tf_op jit(solution)/shard_map/enter_bwd/pallas_call | solution.py:242
  96.1 3.0 %collective-permute-done.20.refs_5_ = bf16[32,7168]{1,0:T(8,128)(2,1)S(1)} collective-permute-done((bf16[32,7168]{1,0:T(8,128)(2,1)S(1)}, bf16[32,7168]{1,0:T(8,128)(2,1)S(1)}, u32[]{:S(2)}, u32[]{:S(2)}) %collective-permute-start.20) | collective-permute-done | bytes 458784 | tf_op jit(solution)/shard_map/ppermute | solution.py:486
  99.0 4.4 %collective-permute-done.18.refs_3_ = bf16[16,7168]{1,0:T(8,128)(2,1)S(1)} collective-permute-done((bf16[16,7168]{1,0:T(8,128)(2,1)S(1)}, bf16[16,7168]{1,0:T(8,128)(2,1)S(1)}, u32[]{:S(2)}, u32[]{:S(2)}) %collective-permute-start.18) | collective-permute-done | bytes 229408 | tf_op jit(solution)/shard_map/ppermute | solution.py:486
  103.4 4.5 %collective-permute-done.19.refs_4_ = bf16[16,7168]{1,0:T(8,128)(2,1)S(1)} collective-permute-done((bf16[16,7168]{1,0:T(8,128)(2,1)S(1)}, bf16[16,7168]{1,0:T(8,128)(2,1)S(1)}, u32[]{:S(2)}, u32[]{:S(2)}) %collective-permute-start.19) | collective-permute-done | bytes 229408 | tf_op jit(solution)/shard_map/ppermute | solution.py:486
  110.0 2.0 %collective-permute-start.36 = (bf16[16,7296]{1,0:T(8,128)(2,1)S(1)}, bf16[16,7296]{1,0:T(8,128)(2,1)S(1)}, u32[]{:S(2)}, u32[]{:S(2)}) collective-permute-start(bf16[16,7296]{1,0:T(8,128)(2,1)S(1)} %get-tuple-element.112), channel_id=1, source_target_pairs={{0,6},{1,7},{2,0},{3,1},{4,2},{5,3},{6,4},{7,5},{8,14},{9,15},{10,... | collective-permute-start | bytes 700424 | tf_op jit(solution)/shard_map/ppermute | solution.py:486
  112.0 4.3 %expert_fwd.1 = (bf16[128,7168]{1,0:T(8,128)(2,1)S(1)}, bf16[128,7168]{1,0:T(8,128)(2,1)S(1)}) custom-call(bf16[32,7168]{1,0:T(8,128)(2,1)S(1)} %bitcast.61, bf16[32,7168]{1,0:T(8,128)(2,1)S(1)} %collective-permute-done.10.refs_1_, bf16[32,7168]{1,0:T(8,128)(2,1)S(1)} %collective-permute-done.11.refs_2_, ...), custom_call_target="tpu_custom_call" | custom-call | flops 1409286144 | bytes 12845056 | tf_op jit(solution)/shard_map/expert_fwd/pallas_call | solution.py:361
  120.7 2.6 %collective-permute-start.26 = (bf16[16,7168]{1,0:T(8,128)(2,1)S(1)}, bf16[16,7168]{1,0:T(8,128)(2,1)S(1)}, u32[]{:S(2)}, u32[]{:S(2)}) collective-permute-start(bf16[16,7168]{1,0:T(8,128)(2,1)S(1)} %get-tuple-element.115), channel_id=1, source_target_pairs={{0,2},{1,3},{2,4},{3,5},{4,6},{5,7},{6,0},{7,1},{8,10},{9,11},{10,... | collective-permute-start | bytes 688136 | tf_op jit(solution)/shard_map/ppermute | solution.py:486
  123.4 3.3 %collective-permute-start.35 = (bf16[32,7296]{1,0:T(8,128)(2,1)S(1)}, bf16[32,7296]{1,0:T(8,128)(2,1)S(1)}, u32[]{:S(2)}, u32[]{:S(2)}) collective-permute-start(bf16[32,7296]{1,0:T(8,128)(2,1)S(1)} %pad_maximum_fusion), channel_id=1, source_target_pairs={{0,2},{1,3},{2,4},{3,5},{4,6},{5,7},{6,0},{7,1},{8,10},{9,11},{10,... | collective-permute-start | bytes 1400840 | tf_op jit(solution)/shard_map/ppermute | solution.py:486
  126.7 2.7 %collective-permute-done.26 = bf16[16,7168]{1,0:T(8,128)(2,1)S(1)} collective-permute-done((bf16[16,7168]{1,0:T(8,128)(2,1)S(1)}, bf16[16,7168]{1,0:T(8,128)(2,1)S(1)}, u32[]{:S(2)}, u32[]{:S(2)}) %collective-permute-start.26) | collective-permute-done | bytes 229408 | tf_op jit(solution)/shard_map/ppermute | solution.py:486
  129.4 8.1 %collective-permute-done.28 = bf16[16,7168]{1,0:T(8,128)(2,1)S(1)} collective-permute-done((bf16[16,7168]{1,0:T(8,128)(2,1)S(1)}, bf16[16,7168]{1,0:T(8,128)(2,1)S(1)}, u32[]{:S(2)}, u32[]{:S(2)}) %collective-permute-start.28) | collective-permute-done | bytes 229408 | tf_op jit(solution)/shard_map/ppermute | solution.py:486
  137.8 3.3 %collective-permute-start.27 = (bf16[32,7168]{1,0:T(8,128)(2,1)S(1)}, bf16[32,7168]{1,0:T(8,128)(2,1)S(1)}, u32[]{:S(2)}, u32[]{:S(2)}) collective-permute-start(bf16[32,7168]{1,0:T(8,128)(2,1)S(1)} %pad_maximum_fusion.2), channel_id=1, source_target_pairs={{0,2},{1,3},{2,4},{3,5},{4,6},{5,7},{6,0},{7,1},{8,10},{9,11},{10,... | collective-permute-start | bytes 1376264 | tf_op jit(solution)/shard_map/ppermute | solution.py:486
  142.1 4.1 %all-to-all-start.2 = ((bf16[4,8,7296]{2,1,0:T(8,128)(2,1)}), bf16[4,8,7296]{2,1,0:T(8,128)(2,1)S(1)}, u32[]{:S(2)}, u32[]{:S(2)}) async-start(bf16[4,8,7296]{2,1,0:T(8,128)(2,1)} %fusion.4), calls=%async_computation.2 | async-start | bytes 933888 | tf_op jit(solution)/shard_map/all_to_all | solution.py:501
  146.2 7.8 %all-to-all-done.2 = bf16[4,8,7296]{2,1,0:T(8,128)(2,1)S(1)} async-done(((bf16[4,8,7296]{2,1,0:T(8,128)(2,1)}), bf16[4,8,7296]{2,1,0:T(8,128)(2,1)S(1)}, u32[]{:S(2)}, u32[]{:S(2)}) %all-to-all-start.2) | async-done | bytes 466976 | tf_op jit(solution)/shard_map/all_to_all | solution.py:501
  155.3 3.6 %collective-permute-start.38 = (bf16[32,7168]{1,0:T(8,128)(2,1)S(1)}, bf16[32,7168]{1,0:T(8,128)(2,1)S(1)}, u32[]{:S(2)}, u32[]{:S(2)}) collective-permute-start(bf16[32,7168]{1,0:T(8,128)(2,1)S(1)} %get-tuple-element.101), channel_id=1, source_target_pairs={{0,224},{32,0},{64,32},{96,64},{128,96},{160,128},{192,160},{224,1... | collective-permute-start | bytes 1376264 | tf_op jit(solution)/shard_map/ppermute | solution.py:491
  162.1 2.6 %collective-permute-start.32 = (bf16[8,7168]{1,0:T(8,128)(2,1)S(1)}, bf16[8,7168]{1,0:T(8,128)(2,1)S(1)}, u32[]{:S(2)}, u32[]{:S(2)}) collective-permute-start(bf16[8,7168]{1,0:T(8,128)(2,1)S(1)} %get-tuple-element.120), channel_id=1, source_target_pairs={{0,48},{1,49},{2,50},{3,51},{4,52},{5,53},{6,54},{7,55},{8,56},{9,... | collective-permute-start | bytes 344072 | tf_op jit(solution)/shard_map/ppermute | solution.py:497
  166.4 4.0 %place_grad.1 = bf16[96,7168]{1,0:T(8,128)(2,1)} custom-call(f32[32,96]{1,0:T(8,128)S(1)} %collective-permute-done.3.first_ref, bf16[48,7168]{1,0:T(8,128)(2,1)S(1)} %copy-done.10, bf16[48,7168]{1,0:T(8,128)(2,1)} %collective-permute-done.7.bottom_ref, bf16[32,7168]{1,0:T(8,128)(2,1)S(1)} %collective-permute-done.38.slots_ref), custom_call_target="tpu_custom_call" | custom-call | flops 88080384 | bytes 4128768 | tf_op jit(solution)/shard_map/place_grad/pallas_call | solution.py:451
  170.5 2.3 %collective-permute-done.33.refs_3_ = bf16[8,7168]{1,0:T(8,128)(2,1)S(1)} collective-permute-done((bf16[8,7168]{1,0:T(8,128)(2,1)S(1)}, bf16[8,7168]{1,0:T(8,128)(2,1)S(1)}, u32[]{:S(2)}, u32[]{:S(2)}) %collective-permute-start.33) | collective-permute-done | bytes 114720 | tf_op jit(solution)/shard_map/ppermute | solution.py:497
  172.9 4.2 %place_fwd.1 = bf16[96,7168]{1,0:T(8,128)(2,1)} custom-call(f32[32,96]{1,0:T(8,128)S(1)} %collective-permute-done.2.mixing_ref, bf16[48,7168]{1,0:T(8,128)(2,1)} %collective-permute-done.top_ref, bf16[48,7168]{1,0:T(8,128)(2,1)} %collective-permute-done.6.bottom_ref, bf16[8,7168]{1,0:T(8,128)(2,1)S(1)} %collective-permute-done.30.refs_0_, ...), custom_call_target="tpu_custom_call" | custom-call | flops 88080384 | bytes 4128768 | tf_op jit(solution)/shard_map/place_fwd/pallas_call | solution.py:451
  (134 shorter events, 49.5 us)
Async XLA Ops:
  9.8 18.4 %all-to-all-start = ((bf16[4,16,7168]{2,1,0:T(8,128)(2,1)}), bf16[4,16,7168]{2,1,0:T(8,128)(2,1)}, u32[]{:S(2)}, u32[]{:S(2)}) async-start(bf16[4,16,7168]{2,1,0:T(8,128)(2,1)} %bitcast.63), calls=%async_computation | async-start | bytes 1835008 | tf_op jit(solution)/shard_map/all_to_all | solution.py:501
  15.3 21.8 %collective-permute-start = (bf16[48,7168]{1,0:T(8,128)(2,1)}, bf16[48,7168]{1,0:T(8,128)(2,1)}, u32[]{:S(2)}, u32[]{:S(2)}) collective-permute-start(bf16[48,7168]{1,0:T(8,128)(2,1)} %slice_bitcast_fusion.1), channel_id=1, source_target_pairs={{0,32},{32,64},{64,96},{96,128},{128,160},{160,192},{192,224},{224... | collective-permute-start | bytes 2064392 | tf_op jit(solution)/shard_map/ppermute | solution.py:491
  18.1 19.0 %collective-permute-start.1 = (bf16[48,7168]{1,0:T(8,128)(2,1)}, bf16[48,7168]{1,0:T(8,128)(2,1)S(1)}, u32[]{:S(2)}, u32[]{:S(2)}) collective-permute-start(bf16[48,7168]{1,0:T(8,128)(2,1)} %slice_bitcast_fusion), channel_id=1, source_target_pairs={{0,224},{32,0},{64,32},{96,64},{128,96},{160,128},{192,160},{224,1... | collective-permute-start | bytes 2064392 | tf_op jit(solution)/shard_map/ppermute | solution.py:491
  24.2 12.7 %collective-permute-start.2 = (f32[32,96]{1,0:T(8,128)S(1)}, f32[32,96]{1,0:T(8,128)S(1)}, u32[]{:S(2)}, u32[]{:S(2)}) collective-permute-start(f32[32,96]{1,0:T(8,128)S(1)} %fusion.9), channel_id=1, source_target_pairs={{0,32},{32,64},{64,96},{96,128},{128,160},{160,192},{192,224},{224... | collective-permute-start | bytes 36872 | tf_op jit(solution)/shard_map/ppermute | solution.py:491
  24.3 12.8 %collective-permute-start.3 = (f32[32,96]{1,0:T(8,128)S(1)}, f32[32,96]{1,0:T(8,128)S(1)}, u32[]{:S(2)}, u32[]{:S(2)}) collective-permute-start(f32[32,96]{1,0:T(8,128)S(1)} %get-tuple-element.56), channel_id=1, source_target_pairs={{0,224},{32,0},{64,32},{96,64},{128,96},{160,128},{192,160},{224,1... | collective-permute-start | bytes 36872 | tf_op jit(solution)/shard_map/ppermute | solution.py:491
  38.0 22.2 %collective-permute-start.4 = (bf16[64,7168]{1,0:T(8,128)(2,1)S(1)}, bf16[64,7168]{1,0:T(8,128)(2,1)}, u32[]{:S(2)}, u32[]{:S(2)}) collective-permute-start(bf16[64,7168]{1,0:T(8,128)(2,1)S(1)} %bitcast.48), channel_id=1, source_target_pairs={{0,2},{1,3},{2,4},{3,5},{4,6},{5,7},{6,0},{7,1},{8,10},{9,11},{10,... | collective-permute-start | bytes 2752520 | tf_op jit(solution)/shard_map/ppermute | solution.py:486
  38.4 22.3 %collective-permute-start.5 = (bf16[64,7168]{1,0:T(8,128)(2,1)S(1)}, bf16[64,7168]{1,0:T(8,128)(2,1)}, u32[]{:S(2)}, u32[]{:S(2)}) collective-permute-start(bf16[64,7168]{1,0:T(8,128)(2,1)S(1)} %bitcast.49), channel_id=1, source_target_pairs={{0,6},{1,7},{2,0},{3,1},{4,2},{5,3},{6,4},{7,5},{8,14},{9,15},{10,... | collective-permute-start | bytes 2752520 | tf_op jit(solution)/shard_map/ppermute | solution.py:486
  40.9 18.0 %collective-permute-start.6 = (bf16[48,7168]{1,0:T(8,128)(2,1)}, bf16[48,7168]{1,0:T(8,128)(2,1)}, u32[]{:S(2)}, u32[]{:S(2)}) collective-permute-start(bf16[48,7168]{1,0:T(8,128)(2,1)} %slice.100), channel_id=1, source_target_pairs={{0,32},{32,64},{64,96},{96,128},{128,160},{160,192},{192,224},{224... | collective-permute-start | bytes 2064392 | tf_op jit(solution)/shard_map/ppermute | solution.py:491
  43.4 16.7 %collective-permute-start.7 = (bf16[48,7168]{1,0:T(8,128)(2,1)}, bf16[48,7168]{1,0:T(8,128)(2,1)}, u32[]{:S(2)}, u32[]{:S(2)}) collective-permute-start(bf16[48,7168]{1,0:T(8,128)(2,1)} %slice.101), channel_id=1, source_target_pairs={{0,224},{32,0},{64,32},{96,64},{128,96},{160,128},{192,160},{224,1... | collective-permute-start | bytes 2064392 | tf_op jit(solution)/shard_map/ppermute | solution.py:491
  46.7 12.2 %all-to-all-start.1 = ((bf16[4,8,7168]{2,1,0:T(8,128)(2,1)}), bf16[4,8,7168]{2,1,0:T(8,128)(2,1)S(1)}, u32[]{:S(2)}, u32[]{:S(2)}) async-start(bf16[4,8,7168]{2,1,0:T(8,128)(2,1)} %bitcast.64), calls=%async_computation.1 | async-start | bytes 917504 | tf_op jit(solution)/shard_map/all_to_all | solution.py:501
  51.2 14.3 %collective-permute-start.12 = (bf16[64,7168]{1,0:T(8,128)(2,1)S(1)}, bf16[64,7168]{1,0:T(8,128)(2,1)}, u32[]{:S(2)}, u32[]{:S(2)}) collective-permute-start(bf16[64,7168]{1,0:T(8,128)(2,1)S(1)} %bitcast.50), channel_id=1, source_target_pairs={{0,1},{1,0},{2,3},{3,2},{4,5},{5,4},{6,7},{7,6},{8,9},{9,8},{10,11... | collective-permute-start | bytes 2752520 | tf_op jit(solution)/shard_map/ppermute | solution.py:486
  63.3 13.5 %collective-permute-start.8 = (bf16[32,7168]{1,0:T(8,128)(2,1)S(1)}, bf16[32,7168]{1,0:T(8,128)(2,1)S(1)}, u32[]{:S(2)}, u32[]{:S(2)}) collective-permute-start(bf16[32,7168]{1,0:T(8,128)(2,1)S(1)} %slice.102), channel_id=1, source_target_pairs={{0,2},{1,3},{2,4},{3,5},{4,6},{5,7},{6,0},{7,1},{8,10},{9,11},{10,... | collective-permute-start | bytes 1376264 | tf_op jit(solution)/shard_map/ppermute | solution.py:486
  64.6 14.6 %collective-permute-start.9 = (bf16[32,7168]{1,0:T(8,128)(2,1)S(1)}, bf16[32,7168]{1,0:T(8,128)(2,1)S(1)}, u32[]{:S(2)}, u32[]{:S(2)}) collective-permute-start(bf16[32,7168]{1,0:T(8,128)(2,1)S(1)} %slice.103), channel_id=1, source_target_pairs={{0,6},{1,7},{2,0},{3,1},{4,2},{5,3},{6,4},{7,5},{8,14},{9,15},{10,... | collective-permute-start | bytes 1376264 | tf_op jit(solution)/shard_map/ppermute | solution.py:486
  65.4 20.2 %collective-permute-start.10 = (bf16[32,7168]{1,0:T(8,128)(2,1)S(1)}, bf16[32,7168]{1,0:T(8,128)(2,1)S(1)}, u32[]{:S(2)}, u32[]{:S(2)}) collective-permute-start(bf16[32,7168]{1,0:T(8,128)(2,1)S(1)} %bitcast.58), channel_id=1, source_target_pairs={{0,2},{1,3},{2,4},{3,5},{4,6},{5,7},{6,0},{7,1},{8,10},{9,11},{10,... | collective-permute-start | bytes 1376264 | tf_op jit(solution)/shard_map/ppermute | solution.py:486
  67.8 20.0 %collective-permute-start.11 = (bf16[32,7168]{1,0:T(8,128)(2,1)S(1)}, bf16[32,7168]{1,0:T(8,128)(2,1)S(1)}, u32[]{:S(2)}, u32[]{:S(2)}) collective-permute-start(bf16[32,7168]{1,0:T(8,128)(2,1)S(1)} %bitcast.59), channel_id=1, source_target_pairs={{0,6},{1,7},{2,0},{3,1},{4,2},{5,3},{6,4},{7,5},{8,14},{9,15},{10,... | collective-permute-start | bytes 1376264 | tf_op jit(solution)/shard_map/ppermute | solution.py:486
  94.5 14.9 %collective-permute-start.17 = (bf16[128,7296]{1,0:T(8,128)(2,1)S(1)}, bf16[128,7296]{1,0:T(8,128)(2,1)S(1)}, u32[]{:S(2)}, u32[]{:S(2)}) collective-permute-start(bf16[128,7296]{1,0:T(8,128)(2,1)S(1)} %get-tuple-element.76), channel_id=1, source_target_pairs={{0,1},{1,0},{2,3},{3,2},{4,5},{5,4},{6,7},{7,6},{8,9},{9,8},{10,11... | collective-permute-start | bytes 5603336 | tf_op jit(solution)/shard_map/ppermute | solution.py:486
  95.1 12.8 %collective-permute-start.21 = (bf16[32,7168]{1,0:T(8,128)(2,1)S(1)}, bf16[32,7168]{1,0:T(8,128)(2,1)S(1)}, u32[]{:S(2)}, u32[]{:S(2)}) collective-permute-start(bf16[32,7168]{1,0:T(8,128)(2,1)S(1)} %collective-permute-done.10.refs_1_), channel_id=1, source_target_pairs={{0,1},{1,0},{2,3},{3,2},{4,5},{5,4},{6,7},{7,6},{8,9},{9,8},{10,11... | collective-permute-start | bytes 1376264 | tf_op jit(solution)/shard_map/ppermute | solution.py:486
  95.3 12.6 %collective-permute-start.22 = (bf16[32,7168]{1,0:T(8,128)(2,1)S(1)}, bf16[32,7168]{1,0:T(8,128)(2,1)S(1)}, u32[]{:S(2)}, u32[]{:S(2)}) collective-permute-start(bf16[32,7168]{1,0:T(8,128)(2,1)S(1)} %collective-permute-done.11.refs_2_), channel_id=1, source_target_pairs={{0,1},{1,0},{2,3},{3,2},{4,5},{5,4},{6,7},{7,6},{8,9},{9,8},{10,11... | collective-permute-start | bytes 1376264 | tf_op jit(solution)/shard_map/ppermute | solution.py:486
  99.0 8.9 %collective-permute-start.19 = (bf16[16,7168]{1,0:T(8,128)(2,1)S(1)}, bf16[16,7168]{1,0:T(8,128)(2,1)S(1)}, u32[]{:S(2)}, u32[]{:S(2)}) collective-permute-start(bf16[16,7168]{1,0:T(8,128)(2,1)S(1)} %slice.105), channel_id=1, source_target_pairs={{0,6},{1,7},{2,0},{3,1},{4,2},{5,3},{6,4},{7,5},{8,14},{9,15},{10,... | collective-permute-start | bytes 688136 | tf_op jit(solution)/shard_map/ppermute | solution.py:486
  110.0 9.0 %collective-permute-start.36 = (bf16[16,7296]{1,0:T(8,128)(2,1)S(1)}, bf16[16,7296]{1,0:T(8,128)(2,1)S(1)}, u32[]{:S(2)}, u32[]{:S(2)}) collective-permute-start(bf16[16,7296]{1,0:T(8,128)(2,1)S(1)} %get-tuple-element.112), channel_id=1, source_target_pairs={{0,6},{1,7},{2,0},{3,1},{4,2},{5,3},{6,4},{7,5},{8,14},{9,15},{10,... | collective-permute-start | bytes 700424 | tf_op jit(solution)/shard_map/ppermute | solution.py:486
  119.2 21.9 %collective-permute-start.37 = (bf16[32,7296]{1,0:T(8,128)(2,1)S(1)}, bf16[32,7296]{1,0:T(8,128)(2,1)S(1)}, u32[]{:S(2)}, u32[]{:S(2)}) collective-permute-start(bf16[32,7296]{1,0:T(8,128)(2,1)S(1)} %pad_maximum_fusion.1), channel_id=1, source_target_pairs={{0,6},{1,7},{2,0},{3,1},{4,2},{5,3},{6,4},{7,5},{8,14},{9,15},{10,... | collective-permute-start | bytes 1400840 | tf_op jit(solution)/shard_map/ppermute | solution.py:486
  120.7 8.7 %collective-permute-start.26 = (bf16[16,7168]{1,0:T(8,128)(2,1)S(1)}, bf16[16,7168]{1,0:T(8,128)(2,1)S(1)}, u32[]{:S(2)}, u32[]{:S(2)}) collective-permute-start(bf16[16,7168]{1,0:T(8,128)(2,1)S(1)} %get-tuple-element.115), channel_id=1, source_target_pairs={{0,2},{1,3},{2,4},{3,5},{4,6},{5,7},{6,0},{7,1},{8,10},{9,11},{10,... | collective-permute-start | bytes 688136 | tf_op jit(solution)/shard_map/ppermute | solution.py:486
  123.4 14.1 %collective-permute-start.28 = (bf16[16,7168]{1,0:T(8,128)(2,1)S(1)}, bf16[16,7168]{1,0:T(8,128)(2,1)S(1)}, u32[]{:S(2)}, u32[]{:S(2)}) collective-permute-start(bf16[16,7168]{1,0:T(8,128)(2,1)S(1)} %get-tuple-element.116), channel_id=1, source_target_pairs={{0,6},{1,7},{2,0},{3,1},{4,2},{5,3},{6,4},{7,5},{8,14},{9,15},{10,... | collective-permute-start | bytes 688136 | tf_op jit(solution)/shard_map/ppermute | solution.py:486
  123.4 17.7 %collective-permute-start.35 = (bf16[32,7296]{1,0:T(8,128)(2,1)S(1)}, bf16[32,7296]{1,0:T(8,128)(2,1)S(1)}, u32[]{:S(2)}, u32[]{:S(2)}) collective-permute-start(bf16[32,7296]{1,0:T(8,128)(2,1)S(1)} %pad_maximum_fusion), channel_id=1, source_target_pairs={{0,2},{1,3},{2,4},{3,5},{4,6},{5,7},{6,0},{7,1},{8,10},{9,11},{10,... | collective-permute-start | bytes 1400840 | tf_op jit(solution)/shard_map/ppermute | solution.py:486
  137.6 21.3 %collective-permute-start.29 = (bf16[32,7168]{1,0:T(8,128)(2,1)S(1)}, bf16[32,7168]{1,0:T(8,128)(2,1)S(1)}, u32[]{:S(2)}, u32[]{:S(2)}) collective-permute-start(bf16[32,7168]{1,0:T(8,128)(2,1)S(1)} %pad_maximum_fusion.3), channel_id=1, source_target_pairs={{0,6},{1,7},{2,0},{3,1},{4,2},{5,3},{6,4},{7,5},{8,14},{9,15},{10,... | collective-permute-start | bytes 1376264 | tf_op jit(solution)/shard_map/ppermute | solution.py:486
  137.8 21.1 %collective-permute-start.27 = (bf16[32,7168]{1,0:T(8,128)(2,1)S(1)}, bf16[32,7168]{1,0:T(8,128)(2,1)S(1)}, u32[]{:S(2)}, u32[]{:S(2)}) collective-permute-start(bf16[32,7168]{1,0:T(8,128)(2,1)S(1)} %pad_maximum_fusion.2), channel_id=1, source_target_pairs={{0,2},{1,3},{2,4},{3,5},{4,6},{5,7},{6,0},{7,1},{8,10},{9,11},{10,... | collective-permute-start | bytes 1376264 | tf_op jit(solution)/shard_map/ppermute | solution.py:486
  142.1 11.9 %all-to-all-start.2 = ((bf16[4,8,7296]{2,1,0:T(8,128)(2,1)}), bf16[4,8,7296]{2,1,0:T(8,128)(2,1)S(1)}, u32[]{:S(2)}, u32[]{:S(2)}) async-start(bf16[4,8,7296]{2,1,0:T(8,128)(2,1)} %fusion.4), calls=%async_computation.2 | async-start | bytes 933888 | tf_op jit(solution)/shard_map/all_to_all | solution.py:501
  155.3 11.0 %collective-permute-start.38 = (bf16[32,7168]{1,0:T(8,128)(2,1)S(1)}, bf16[32,7168]{1,0:T(8,128)(2,1)S(1)}, u32[]{:S(2)}, u32[]{:S(2)}) collective-permute-start(bf16[32,7168]{1,0:T(8,128)(2,1)S(1)} %get-tuple-element.101), channel_id=1, source_target_pairs={{0,224},{32,0},{64,32},{96,64},{128,96},{160,128},{192,160},{224,1... | collective-permute-start | bytes 1376264 | tf_op jit(solution)/shard_map/ppermute | solution.py:491
  160.3 10.1 %collective-permute-start.30 = (bf16[8,7168]{1,0:T(8,128)(2,1)S(1)}, bf16[8,7168]{1,0:T(8,128)(2,1)S(1)}, u32[]{:S(2)}, u32[]{:S(2)}) collective-permute-start(bf16[8,7168]{1,0:T(8,128)(2,1)S(1)} %get-tuple-element.122), channel_id=1, source_target_pairs={{0,32},{32,64},{64,96},{96,128},{128,160},{160,192},{192,224},{224... | collective-permute-start | bytes 344072 | tf_op jit(solution)/shard_map/ppermute | solution.py:491
  160.4 10.0 %collective-permute-start.31 = (bf16[8,7168]{1,0:T(8,128)(2,1)S(1)}, bf16[8,7168]{1,0:T(8,128)(2,1)S(1)}, u32[]{:S(2)}, u32[]{:S(2)}) collective-permute-start(bf16[8,7168]{1,0:T(8,128)(2,1)S(1)} %get-tuple-element.121), channel_id=1, source_target_pairs={{0,56},{1,57},{2,58},{3,59},{4,60},{5,61},{6,62},{7,63},{8,32},{9,... | collective-permute-start | bytes 344072 | tf_op jit(solution)/shard_map/ppermute | solution.py:497
  162.1 8.4 %collective-permute-start.32 = (bf16[8,7168]{1,0:T(8,128)(2,1)S(1)}, bf16[8,7168]{1,0:T(8,128)(2,1)S(1)}, u32[]{:S(2)}, u32[]{:S(2)}) collective-permute-start(bf16[8,7168]{1,0:T(8,128)(2,1)S(1)} %get-tuple-element.120), channel_id=1, source_target_pairs={{0,48},{1,49},{2,50},{3,51},{4,52},{5,53},{6,54},{7,55},{8,56},{9,... | collective-permute-start | bytes 344072 | tf_op jit(solution)/shard_map/ppermute | solution.py:497
  164.7 8.1 %collective-permute-start.33 = (bf16[8,7168]{1,0:T(8,128)(2,1)S(1)}, bf16[8,7168]{1,0:T(8,128)(2,1)S(1)}, u32[]{:S(2)}, u32[]{:S(2)}) collective-permute-start(bf16[8,7168]{1,0:T(8,128)(2,1)S(1)} %get-tuple-element.119), channel_id=1, source_target_pairs={{0,40},{1,41},{2,42},{3,43},{4,44},{5,45},{6,46},{7,47},{8,48},{9,... | collective-permute-start | bytes 344072 | tf_op jit(solution)/shard_map/ppermute | solution.py:497
  (35 other events, 242.5 us)

commit v2 on v1

--- a/solution.py
+++ b/solution.py
@@ -13,14 +13,14 @@
 LANES = 128
 EPSILON = 1e-06
 ROUTE_SCALE = 2.5
-VMEM_LIMIT = 24 * 1024 * 1024
+MIB = 1024 * 1024
 
 bf16 = jnp.bfloat16
 f32 = jnp.float32
 
 
-def params():
-    return pltpu.CompilerParams(vmem_limit_bytes=VMEM_LIMIT)
+def params(mib=24):
+    return pltpu.CompilerParams(vmem_limit_bytes=mib * MIB)
 
 
 def cost(flops, bytes_accessed):
@@ -160,7 +160,7 @@
 def prep_bwd(routes, scores, x, cot, gain, window):
     rows, width = x.shape
     slots = window * CAP
-    steps = 4
+    steps = 2
     block = width // steps
     shapes = [
         ((2 * slots, width), bf16),
@@ -184,7 +184,7 @@
             pltpu.VMEM((slots, width), f32),
             pltpu.VMEM((slots, width), f32),
         ],
-        compiler_params=params(),
+        compiler_params=params(60),
         cost_estimate=cost(4 * slots * rows * width, 8 * rows * width),
         name="prep_bwd",
     )(routes, scores, x, cot, gain)
@@ -193,7 +193,7 @@
 def prep_fwd(routes, scores, x, gain, window):
     rows, width = x.shape
     slots = window * CAP
-    steps = 4
+    steps = 2
     block = width // steps
     return pl.pallas_call(
         functools.partial(prep_fwd_kernel, steps),
@@ -206,7 +206,7 @@
         + [across(rows, block), whole(gain.shape)],
         out_specs=[whole((slots, width)), whole((slots, rows))],
         scratch_shapes=[pltpu.VMEM((slots, rows), bf16), pltpu.VMEM((slots, width), f32)],
-        compiler_params=params(),
+        compiler_params=params(60),
         cost_estimate=cost(2 * slots * rows * width, 4 * rows * width),
         name="prep_fwd",
     )(routes, scores, x, gain)
@@ -234,7 +234,7 @@
 
 def enter_bwd(cots, inputs, gate, up, down):
     width, hidden = gate.shape
-    steps = 4
+    steps = 2
     block = width // steps
     part = 32
     total = len(cots) * part
@@ -297,7 +297,7 @@
 
 def leave_bwd(near, far, gate, up):
     width, hidden = gate.shape
-    steps = 4
+    steps = 2
     block = width // steps
     total = near[1].shape[0] + far[1].shape[0]
     out = jax.ShapeDtypeStruct((total // 2, width + LANES), bf16)
@@ -352,7 +352,7 @@
 
 def expert_fwd(own, peer, gate, up, down):
     width, hidden = gate.shape
-    steps = 4
+    steps = 2
     block = width // steps
     chunks = own + peer
     rows = sum(c.shape[0] for c in own)
@@ -433,20 +433,20 @@
     out_ref[...] = jnp.where(touched > 0.0, placed, stacked([top_ref, bottom_ref])).astype(bf16)
 
 
-def place_fwd_kernel(mixing_ref, top_ref, bottom_ref, *refs):
+def place_fwd_kernel(mixing_ref, early_ref, *refs):
     out_ref = refs[-1]
     mixing = mixing_ref[...]
     high = mixing.astype(bf16)
     low = (mixing - high.astype(f32)).astype(bf16)
     rows = stacked(refs[:-1]).astype(bf16)
     branch = dot(high, rows, ((0,), (0,))) + dot(low, rows, ((0,), (0,)))
-    out_ref[...] = (stacked([top_ref, bottom_ref]) + branch).astype(bf16)
+    out_ref[...] = (early_ref[...].astype(f32) + branch).astype(bf16)
 
 
 def place(kernel, name, table, early, *blocks):
     slots, rows = table.shape
     width = early[0].shape[1]
-    steps = 4
+    steps = 2
     block = width // steps
     return pl.pallas_call(
         kernel,
@@ -563,41 +563,37 @@
 
     mine_b = net.exchange(cb).reshape(window, 2, CAP, width)
     mine_b = mine_b.transpose(1, 0, 2, 3).reshape(cb.shape)
-    top_f = net.relay(x_f[:middle], 1)
+    mine_b, rows_f = lax.optimization_barrier((mine_b, rows_f))
+
+    left_b, right_b = net.near(mine_b)
+    mine_f = net.exchange(rows_f)
+    early_f = net.relay(x_f, 1)
     top_c = net.relay(cot[:middle], -1)
     mixing = block_of(jnp.concatenate([mixing, mixing], axis=0), row, CAP, window)
     mixing = net.relay(mixing, 1)
     first = net.relay(first, -1)
-    mine_b, rows_f, top_f, top_c, mixing, first = lax.optimization_barrier(
-        (mine_b, rows_f, top_f, top_c, mixing, first)
-    )
-
-    left_b, right_b = net.near(mine_b)
-    mine_f = net.exchange(rows_f)
-    bottom_f = net.relay(after(x_f, rows_f)[middle:], 1)
-    bottom_c = net.relay(after(cot, rows_f)[middle:], -1)
-    left_b, right_b, mine_f, bottom_f, bottom_c = lax.optimization_barrier(
-        (left_b, right_b, mine_f, bottom_f, bottom_c)
+    left_b, right_b, mine_f, early_f, top_c, mixing, first = lax.optimization_barrier(
+        (left_b, right_b, mine_f, early_f, top_c, mixing, first)
     )
 
     far_b = net.far(left_b, right_b)
     near_f = net.near(mine_f)
     near_b = [mine_b, left_b, right_b]
     near_b = near_b + net.swap(near_b)
+    bottom_c = net.relay(after(cot, near_b[5])[middle:], -1)
     near_h = enter_bwd([(a, 0) for a in near_b], [(a, 1) for a in near_b], gate, up, down)
-    far_b, near_f, near_h = lax.optimization_barrier((far_b, near_f, near_h))
+    far_b, near_f, near_h, bottom_c = lax.optimization_barrier((far_b, near_f, near_h, bottom_c))
 
     far_f = net.far(*near_f)
-    own_f = [mine_f, *near_f, *far_f]
     far_b = [*far_b, *net.swap(far_b)]
     far_h = enter_bwd([(a, 0) for a in far_b[0::2]], [(a, 0) for a in far_b[1::2]], gate, up, down)
     own, peer = leave_bwd(near_h, far_h, gate, up)
     other = net.move(peer, dc=1)
-    peer_f = net.swap(own_f)
-    own, other, own_f, peer_f = lax.optimization_barrier((own, other, own_f, peer_f))
+    own, other, far_f = lax.optimization_barrier((own, other, far_f))
 
     dn = net.exchange(net.collect(own, other))
-    own, peer = expert_fwd(own_f, peer_f, gate, up, down)
+    own_f = [mine_f, *near_f, *far_f]
+    own, peer = expert_fwd(own_f, net.swap(own_f), gate, up, down)
     outs = net.collect(own, net.move(peer, dc=1))
     outs = [
         net.relay(block_of(outs, lax.rem(row + window - d, window), CAP), 1, dy=-d)
@@ -607,7 +603,7 @@
         routes_b, scores_b, table, weights, inverse, xs, cs, gain, dn
     )
     late_b = net.relay(grads, -1)
-    fwd_handoff = place(place_fwd_kernel, "place_fwd", mixing, (top_f, bottom_f), *outs)
+    fwd_handoff = place(place_fwd_kernel, "place_fwd", mixing, (early_f,), *outs)
     grad_handoff = place(place_grad_kernel, "place_grad", first, (top_c, bottom_c), late_b)
     return (fwd_handoff[None], grad_handoff[None], score_rows.T[None])
 

time: 178 us -> 162 us (0.910)
  local copies, waits for them, and re-layouts: 18.8 us -> 7.47 us
  starting transfers between devices: 57 us -> 49.8 us
  waiting for transfers between devices: 71.4 us -> 76.1 us
  Pallas kernels: 25.4 us -> 23.6 us
    unnamed x50 -> x38, local copies, waits for them, and re-layouts: 10.4 us -> 3.08 us
    ppermute x8 -> x7, waiting for transfers between devices: 8.92 us -> 15.7 us  [relay(): return lax.ppermute(array, 'section', pairs)]
    ppermute x3, starting transfers between devices: 5.99 us -> 2.81 us  [relay(): return lax.ppermute(array, ('section', 'expert'), pairs)]
    slice x3 -> x1, local copies, waits for them, and re-layouts: 3.96 us -> 1.14 us  [per_device(): bottom_c = net.relay(after(cot, near_b[5])[middle:], -1)]
    pallas_call x2, Pallas kernels: 8.22 us -> 5.66 us  [place(): pl.pallas_call(kernel, out_shape=jax.ShapeDtypeStruct((rows, width), bf16...]
    ppermute x28, waiting for transfers between devices: 43.7 us -> 41.3 us  [move(): return lax.ppermute(array, 'expert', self.pairs(dy, dx, dc))]
    pallas_call x1, Pallas kernels: 1.86 us -> 3.92 us  [prep_bwd(): pl.pallas_call(functools.partial(prep_bwd_kernel, steps), out_shape=[jax....]
    ppermute x8 -> x7, starting transfers between devices: 16.5 us -> 14.7 us  [relay(): return lax.ppermute(array, 'section', pairs)]
  transfers between devices with their start and end apart: 42 -> 41, of which waited for: 24 -> 20; matrix products, arithmetic and copies ran while one was open for 6% -> 5% of each run, Pallas kernels for 9% -> 8%
where the time goes in v2:
time: 162 us
  waiting for transfers between devices  76.1 us (47%)
  starting transfers between devices  49.8 us (31%)
  Pallas kernels  23.6 us (15%)
  local copies, waits for them, and re-layouts  7.47 us (5%)
  other arithmetic  3.55 us (2%)
    ppermute x28, waiting for transfers between devices, move(): return lax.ppermute(array, 'expert', self.pairs(dy, dx, dc))  41.3 us
    ppermute x28, starting transfers between devices, move(): return lax.ppermute(array, 'expert', self.pairs(dy, dx, dc))  19.8 us
    all_to_all x3, waiting for transfers between devices, exchange(): lax.all_to_all(blocks, 'expert', 0, 0, tiled=True, axis_index_groups=self...  17 us
    ppermute x7, waiting for transfers between devices, relay(): return lax.ppermute(array, 'section', pairs)  15.7 us
    ppermute x7, starting transfers between devices, relay(): return lax.ppermute(array, 'section', pairs)  14.7 us
    all_to_all x3, starting transfers between devices, exchange(): lax.all_to_all(blocks, 'expert', 0, 0, tiled=True, axis_index_groups=self...  12.5 us
    pallas_call x2, Pallas kernels, place(): pl.pallas_call(kernel, out_shape=jax.ShapeDtypeStruct((rows, width), bf16...  5.66 us
    pallas_call x2, Pallas kernels, enter_bwd(): pl.pallas_call(functools.partial(enter_bwd_kernel, steps, len(cots)), out...  4.96 us
  transfers between devices with their start and end apart: 41, of which 20 were waited for; matrix products, arithmetic and copies ran while one was open for 5% of the time, Pallas kernels for 8%

profile of v2, /device:TPU:6, one launch (start us, length us, event | category | flops | bytes accessed | tf_op | source)
XLA Modules:
  0.0 161.5 jit_solution(9311834647434783720)
XLA Ops:
  0.6 3.9 %prep_bwd.1 = (bf16[64,7168]{1,0:T(8,128)(2,1)}, bf16[32,7168]{1,0:T(8,128)(2,1)}, bf16[32,7168]{1,0:T(8,128)(2,1)}, f32[32,96]{1,0:T(8,128)}, f32[32,96]{1,0:T(...) custom-call(s32[8,96]{1,0:T(8,128)} %bitcast.56, f32[8,96]{1,0:T(8,128)} %bitcast.58, bf16[96,7168]{1,0:T(8,128)(2,1)} %bitcast.63, ...), custom_call_target="tpu_custom_call" | custom-call | flops 88080384 | bytes 5505024 | tf_op jit(solution)/shard_map/prep_bwd/pallas_call | solution.py:174
  4.6 4.5 %all-to-all-start = ((bf16[4,16,7168]{2,1,0:T(8,128)(2,1)}), bf16[4,16,7168]{2,1,0:T(8,128)(2,1)S(1)}, u32[]{:S(2)}, u32[]{:S(2)}) async-start(bf16[4,16,7168]{2,1,0:T(8,128)(2,1)} %bitcast.68), calls=%async_computation | async-start | bytes 1835008 | tf_op jit(solution)/shard_map/all_to_all | solution.py:501
  9.0 1.9 %collective-permute-start.2 = (bf16[96,7168]{1,0:T(8,128)(2,1)}, bf16[96,7168]{1,0:T(8,128)(2,1)}, u32[]{:S(2)}, u32[]{:S(2)}) collective-permute-start(bf16[96,7168]{1,0:T(8,128)(2,1)} %bitcast.64), channel_id=1, source_target_pairs={{0,32},{32,64},{64,96},{96,128},{128,160},{160,192},{192,224},{224... | collective-permute-start | bytes 4128776 | tf_op jit(solution)/shard_map/ppermute | solution.py:491
  11.0 2.8 %prep_fwd.1 = (bf16[32,7168]{1,0:T(8,128)(2,1)}, f32[32,96]{1,0:T(8,128)}) custom-call(s32[8,96]{1,0:T(8,128)} %bitcast.70, f32[8,96]{1,0:T(8,128)} %bitcast.71, bf16[96,7168]{1,0:T(8,128)(2,1)} %bitcast.65, f32[1,7168]{1,0:T(1,128)} %gain_ref.5), custom_call_target="tpu_custom_call" | custom-call | flops 44040192 | bytes 2752512 | tf_op jit(solution)/shard_map/prep_fwd/pallas_call | solution.py:198
  13.8 9.0 %all-to-all-done = bf16[4,16,7168]{2,1,0:T(8,128)(2,1)S(1)} async-done(((bf16[4,16,7168]{2,1,0:T(8,128)(2,1)}), bf16[4,16,7168]{2,1,0:T(8,128)(2,1)S(1)}, u32[]{:S(2)}, u32[]{:S(2)}) %all-to-all-start) | async-done | bytes 917536 | tf_op jit(solution)/shard_map/all_to_all | solution.py:501
  25.8 5.8 %collective-permute-start.3 = (bf16[48,7168]{1,0:T(8,128)(2,1)}, bf16[48,7168]{1,0:T(8,128)(2,1)}, u32[]{:S(2)}, u32[]{:S(2)}) collective-permute-start(bf16[48,7168]{1,0:T(8,128)(2,1)} %slice_bitcast_fusion), channel_id=1, source_target_pairs={{0,224},{32,0},{64,32},{96,64},{128,96},{160,128},{192,160},{224,1... | collective-permute-start | bytes 2064392 | tf_op jit(solution)/shard_map/ppermute | solution.py:491
  31.6 3.5 %all-to-all-start.1 = ((bf16[4,8,7168]{2,1,0:T(8,128)(2,1)}), bf16[4,8,7168]{2,1,0:T(8,128)(2,1)S(1)}, u32[]{:S(2)}, u32[]{:S(2)}) async-start(bf16[4,8,7168]{2,1,0:T(8,128)(2,1)} %bitcast.69), calls=%async_computation.1 | async-start | bytes 917504 | tf_op jit(solution)/shard_map/all_to_all | solution.py:501
  35.3 10.1 %collective-permute-done.4.mixing_ref = f32[32,96]{1,0:T(8,128)S(1)} collective-permute-done((f32[32,96]{1,0:T(8,128)S(1)}, f32[32,96]{1,0:T(8,128)S(1)}, u32[]{:S(2)}, u32[]{:S(2)}) %collective-permute-start.4) | collective-permute-done | bytes 12320 | tf_op jit(solution)/shard_map/ppermute | solution.py:491
  45.4 1.7 %collective-permute-start.5 = (f32[32,96]{1,0:T(8,128)S(1)}, f32[32,96]{1,0:T(8,128)S(1)}, u32[]{:S(2)}, u32[]{:S(2)}) collective-permute-start(f32[32,96]{1,0:T(8,128)S(1)} %copy-done.18), channel_id=1, source_target_pairs={{0,224},{32,0},{64,32},{96,64},{128,96},{160,128},{192,160},{224,1... | collective-permute-start | bytes 36872 | tf_op jit(solution)/shard_map/ppermute | solution.py:491
  47.1 2.0 %collective-permute-done.5.first_ref = f32[32,96]{1,0:T(8,128)S(1)} collective-permute-done((f32[32,96]{1,0:T(8,128)S(1)}, f32[32,96]{1,0:T(8,128)S(1)}, u32[]{:S(2)}, u32[]{:S(2)}) %collective-permute-start.5) | collective-permute-done | bytes 12320 | tf_op jit(solution)/shard_map/ppermute | solution.py:491
  49.8 2.4 %collective-permute-done.12.refs_5_.refs_11_ = bf16[64,7168]{1,0:T(8,128)(2,1)S(1)} collective-permute-done((bf16[64,7168]{1,0:T(8,128)(2,1)}, bf16[64,7168]{1,0:T(8,128)(2,1)S(1)}, u32[]{:S(2)}, u32[]{:S(2)}) %collective-permute-start.12) | collective-permute-done | bytes 917536 | tf_op jit(solution)/shard_map/ppermute | solution.py:486
  53.4 3.0 %collective-permute-start.13 = (bf16[48,7168]{1,0:T(8,128)(2,1)S(1)}, bf16[48,7168]{1,0:T(8,128)(2,1)S(1)}, u32[]{:S(2)}, u32[]{:S(2)}) collective-permute-start(bf16[48,7168]{1,0:T(8,128)(2,1)S(1)} %slice.91), channel_id=1, source_target_pairs={{0,224},{32,0},{64,32},{96,64},{128,96},{160,128},{192,160},{224,1... | collective-permute-start | bytes 2064392 | tf_op jit(solution)/shard_map/ppermute | solution.py:491
  65.6 3.2 %enter_bwd.2 = (f32[192,256]{1,0:T(8,128)S(1)}, f32[192,128]{1,0:T(8,128)S(1)}) custom-call(bf16[64,7168]{1,0:T(8,128)(2,1)S(1)} %bitcast.49, bf16[64,7168]{1,0:T(8,128)(2,1)} %collective-permute-done.refs_1_.refs_7_, bf16[64,7168]{1,0:T(8,128)(2,1)} %collective-permute-done.1.refs_2_.refs_8_, bf16[64,7168]{1,0:T(8,128)(2,1)S(1)} %collective-permute-done.10.refs_3_.refs_9_, ...), custom_call_target="tpu_custom_call" | custom-call | flops 1056964608 | bytes 11010048 | tf_op jit(solution)/shard_map/enter_bwd/pallas_call | solution.py:242
  68.8 3.2 %collective-permute-done.6.refs_0_ = bf16[32,7168]{1,0:T(8,128)(2,1)S(1)} collective-permute-done((bf16[32,7168]{1,0:T(8,128)(2,1)S(1)}, bf16[32,7168]{1,0:T(8,128)(2,1)S(1)}, u32[]{:S(2)}, u32[]{:S(2)}) %collective-permute-start.6) | collective-permute-done | bytes 458784 | tf_op jit(solution)/shard_map/ppermute | solution.py:486
  72.0 1.7 %collective-permute-done.7.refs_2_ = bf16[32,7168]{1,0:T(8,128)(2,1)S(1)} collective-permute-done((bf16[32,7168]{1,0:T(8,128)(2,1)S(1)}, bf16[32,7168]{1,0:T(8,128)(2,1)S(1)}, u32[]{:S(2)}, u32[]{:S(2)}) %collective-permute-start.7) | collective-permute-done | bytes 458784 | tf_op jit(solution)/shard_map/ppermute | solution.py:486
  73.7 7.0 %collective-permute-done.8.refs_1_ = bf16[32,7168]{1,0:T(8,128)(2,1)S(1)} collective-permute-done((bf16[32,7168]{1,0:T(8,128)(2,1)S(1)}, bf16[32,7168]{1,0:T(8,128)(2,1)S(1)}, u32[]{:S(2)}, u32[]{:S(2)}) %collective-permute-start.8) | collective-permute-done | bytes 458784 | tf_op jit(solution)/shard_map/ppermute | solution.py:486
  84.6 1.8 %enter_bwd.3 = (f32[64,256]{1,0:T(8,128)S(1)}, f32[64,128]{1,0:T(8,128)S(1)}) custom-call(bf16[32,7168]{1,0:T(8,128)(2,1)S(1)} %collective-permute-done.6.refs_0_, bf16[32,7168]{1,0:T(8,128)(2,1)S(1)} %collective-permute-done.14.refs_1_, bf16[32,7168]{1,0:T(8,128)(2,1)S(1)} %collective-permute-done.7.refs_2_, ...), custom_call_target="tpu_custom_call" | custom-call | flops 352321536 | bytes 7340032 | tf_op jit(solution)/shard_map/enter_bwd/pallas_call | solution.py:242
  88.7 1.7 %collective-permute-start.18 = (bf16[16,7168]{1,0:T(8,128)(2,1)S(1)}, bf16[16,7168]{1,0:T(8,128)(2,1)S(1)}, u32[]{:S(2)}, u32[]{:S(2)}) collective-permute-start(bf16[16,7168]{1,0:T(8,128)(2,1)S(1)} %slice.93), channel_id=1, source_target_pairs={{0,6},{1,7},{2,0},{3,1},{4,2},{5,3},{6,4},{7,5},{8,14},{9,15},{10,... | collective-permute-start | bytes 688136 | tf_op jit(solution)/shard_map/ppermute | solution.py:486
  90.9 5.2 %collective-permute-done.17.refs_3_ = bf16[16,7168]{1,0:T(8,128)(2,1)S(1)} collective-permute-done((bf16[16,7168]{1,0:T(8,128)(2,1)S(1)}, bf16[16,7168]{1,0:T(8,128)(2,1)S(1)}, u32[]{:S(2)}, u32[]{:S(2)}) %collective-permute-start.17) | collective-permute-done | bytes 229408 | tf_op jit(solution)/shard_map/ppermute | solution.py:486
  99.0 1.7 %collective-permute-start.35 = (bf16[16,7296]{1,0:T(8,128)(2,1)S(1)}, bf16[16,7296]{1,0:T(8,128)(2,1)S(1)}, u32[]{:S(2)}, u32[]{:S(2)}) collective-permute-start(bf16[16,7296]{1,0:T(8,128)(2,1)S(1)} %get-tuple-element.92), channel_id=1, source_target_pairs={{0,6},{1,7},{2,0},{3,1},{4,2},{5,3},{6,4},{7,5},{8,14},{9,15},{10,... | collective-permute-start | bytes 700424 | tf_op jit(solution)/shard_map/ppermute | solution.py:486
  100.7 3.3 %expert_fwd.1 = (bf16[128,7168]{1,0:T(8,128)(2,1)S(1)}, bf16[128,7168]{1,0:T(8,128)(2,1)S(1)}) custom-call(bf16[32,7168]{1,0:T(8,128)(2,1)S(1)} %bitcast.55, bf16[32,7168]{1,0:T(8,128)(2,1)S(1)} %collective-permute-done.8.refs_1_, bf16[32,7168]{1,0:T(8,128)(2,1)S(1)} %collective-permute-done.9.refs_2_, bf16[16,7168]{1,0:T(8,128)(2,1)S(1)} %collective-permute-done.17.refs_3_, ...), custom_call_target="tpu_custom_call" | custom-call | flops 1409286144 | bytes 12845056 | tf_op jit(solution)/shard_map/expert_fwd/pallas_call | solution.py:361
  104.4 1.9 %collective-permute-done.33 = bf16[16,7296]{1,0:T(8,128)(2,1)S(1)} collective-permute-done((bf16[16,7296]{1,0:T(8,128)(2,1)S(1)}, bf16[16,7296]{1,0:T(8,128)(2,1)S(1)}, u32[]{:S(2)}, u32[]{:S(2)}) %collective-permute-start.33) | collective-permute-done | bytes 233504 | tf_op jit(solution)/shard_map/ppermute | solution.py:486
  111.2 1.8 %collective-permute-start.36 = (bf16[32,7296]{1,0:T(8,128)(2,1)S(1)}, bf16[32,7296]{1,0:T(8,128)(2,1)S(1)}, u32[]{:S(2)}, u32[]{:S(2)}) collective-permute-start(bf16[32,7296]{1,0:T(8,128)(2,1)S(1)} %pad_maximum_fusion.1), channel_id=1, source_target_pairs={{0,6},{1,7},{2,0},{3,1},{4,2},{5,3},{6,4},{7,5},{8,14},{9,15},{10,... | collective-permute-start | bytes 1400840 | tf_op jit(solution)/shard_map/ppermute | solution.py:486
  113.0 12.0 %collective-permute-done.25 = bf16[16,7168]{1,0:T(8,128)(2,1)S(1)} collective-permute-done((bf16[16,7168]{1,0:T(8,128)(2,1)S(1)}, bf16[16,7168]{1,0:T(8,128)(2,1)S(1)}, u32[]{:S(2)}, u32[]{:S(2)}) %collective-permute-start.25) | collective-permute-done | bytes 229408 | tf_op jit(solution)/shard_map/ppermute | solution.py:486
  125.1 1.9 %collective-permute-start.26 = (bf16[32,7168]{1,0:T(8,128)(2,1)S(1)}, bf16[32,7168]{1,0:T(8,128)(2,1)S(1)}, u32[]{:S(2)}, u32[]{:S(2)}) collective-permute-start(bf16[32,7168]{1,0:T(8,128)(2,1)S(1)} %pad_maximum_fusion.2), channel_id=1, source_target_pairs={{0,2},{1,3},{2,4},{3,5},{4,6},{5,7},{6,0},{7,1},{8,10},{9,11},{10,... | collective-permute-start | bytes 1376264 | tf_op jit(solution)/shard_map/ppermute | solution.py:486
  129.9 4.5 %all-to-all-start.2 = ((bf16[4,8,7296]{2,1,0:T(8,128)(2,1)}), bf16[4,8,7296]{2,1,0:T(8,128)(2,1)S(1)}, u32[]{:S(2)}, u32[]{:S(2)}) async-start(bf16[4,8,7296]{2,1,0:T(8,128)(2,1)} %fusion.4), calls=%async_computation.2 | async-start | bytes 933888 | tf_op jit(solution)/shard_map/all_to_all | solution.py:501
  134.4 8.0 %all-to-all-done.2 = bf16[4,8,7296]{2,1,0:T(8,128)(2,1)S(1)} async-done(((bf16[4,8,7296]{2,1,0:T(8,128)(2,1)}), bf16[4,8,7296]{2,1,0:T(8,128)(2,1)S(1)}, u32[]{:S(2)}, u32[]{:S(2)}) %all-to-all-start.2) | async-done | bytes 466976 | tf_op jit(solution)/shard_map/all_to_all | solution.py:501
  145.5 1.8 %collective-permute-start.29 = (bf16[8,7168]{1,0:T(8,128)(2,1)S(1)}, bf16[8,7168]{1,0:T(8,128)(2,1)S(1)}, u32[]{:S(2)}, u32[]{:S(2)}) collective-permute-start(bf16[8,7168]{1,0:T(8,128)(2,1)S(1)} %get-tuple-element.102), channel_id=1, source_target_pairs={{0,32},{32,64},{64,96},{96,128},{128,160},{160,192},{192,224},{224... | collective-permute-start | bytes 344072 | tf_op jit(solution)/shard_map/ppermute | solution.py:491
  148.2 2.0 %collective-permute-start.32 = (bf16[8,7168]{1,0:T(8,128)(2,1)S(1)}, bf16[8,7168]{1,0:T(8,128)(2,1)S(1)}, u32[]{:S(2)}, u32[]{:S(2)}) collective-permute-start(bf16[8,7168]{1,0:T(8,128)(2,1)S(1)} %get-tuple-element.99), channel_id=1, source_target_pairs={{0,40},{1,41},{2,42},{3,43},{4,44},{5,45},{6,46},{7,47},{8,48},{9,... | collective-permute-start | bytes 344072 | tf_op jit(solution)/shard_map/ppermute | solution.py:497
  150.1 3.6 %collective-permute-done.37.slots_ref = bf16[32,7168]{1,0:T(8,128)(2,1)S(1)} collective-permute-done((bf16[32,7168]{1,0:T(8,128)(2,1)S(1)}, bf16[32,7168]{1,0:T(8,128)(2,1)S(1)}, u32[]{:S(2)}, u32[]{:S(2)}) %collective-permute-start.37) | collective-permute-done | bytes 458784 | tf_op jit(solution)/shard_map/ppermute | solution.py:491
  153.7 2.6 %place_grad.1 = bf16[96,7168]{1,0:T(8,128)(2,1)} custom-call(f32[32,96]{1,0:T(8,128)S(1)} %collective-permute-done.5.first_ref, bf16[48,7168]{1,0:T(8,128)(2,1)} %collective-permute-done.3.top_ref, bf16[48,7168]{1,0:T(8,128)(2,1)S(1)} %copy-done.6, bf16[32,7168]{1,0:T(8,128)(2,1)S(1)} %collective-permute-done.37.slots_ref), custom_call_target="tpu_custom_call" | custom-call | flops 88080384 | bytes 4128768 | tf_op jit(solution)/shard_map/place_grad/pallas_call | solution.py:451
  158.5 3.0 %place_fwd.1 = bf16[96,7168]{1,0:T(8,128)(2,1)} custom-call(f32[32,96]{1,0:T(8,128)S(1)} %collective-permute-done.4.mixing_ref, bf16[96,7168]{1,0:T(8,128)(2,1)} %collective-permute-done.2.early_ref, bf16[8,7168]{1,0:T(8,128)(2,1)S(1)} %collective-permute-done.29.refs_0_, bf16[8,7168]{1,0:T(8,128)(2,1)S(1)} %collective-permute-done.30.refs_1_, ...), custom_call_target="tpu_custom_call" | custom-call | flops 88080384 | bytes 4128768 | tf_op jit(solution)/shard_map/place_fwd/pallas_call | solution.py:451
  (118 shorter events, 37.8 us)
Async XLA Ops:
  4.6 18.2 %all-to-all-start = ((bf16[4,16,7168]{2,1,0:T(8,128)(2,1)}), bf16[4,16,7168]{2,1,0:T(8,128)(2,1)S(1)}, u32[]{:S(2)}, u32[]{:S(2)}) async-start(bf16[4,16,7168]{2,1,0:T(8,128)(2,1)} %bitcast.68), calls=%async_computation | async-start | bytes 1835008 | tf_op jit(solution)/shard_map/all_to_all | solution.py:501
  9.0 40.1 %collective-permute-start.2 = (bf16[96,7168]{1,0:T(8,128)(2,1)}, bf16[96,7168]{1,0:T(8,128)(2,1)}, u32[]{:S(2)}, u32[]{:S(2)}) collective-permute-start(bf16[96,7168]{1,0:T(8,128)(2,1)} %bitcast.64), channel_id=1, source_target_pairs={{0,32},{32,64},{64,96},{96,128},{128,160},{160,192},{192,224},{224... | collective-permute-start | bytes 4128776 | tf_op jit(solution)/shard_map/ppermute | solution.py:491
  22.8 26.3 %collective-permute-start = (bf16[64,7168]{1,0:T(8,128)(2,1)S(1)}, bf16[64,7168]{1,0:T(8,128)(2,1)}, u32[]{:S(2)}, u32[]{:S(2)}) collective-permute-start(bf16[64,7168]{1,0:T(8,128)(2,1)S(1)} %bitcast.46), channel_id=1, source_target_pairs={{0,2},{1,3},{2,4},{3,5},{4,6},{5,7},{6,0},{7,1},{8,10},{9,11},{10,... | collective-permute-start | bytes 2752520 | tf_op jit(solution)/shard_map/ppermute | solution.py:486
  23.4 25.8 %collective-permute-start.1 = (bf16[64,7168]{1,0:T(8,128)(2,1)S(1)}, bf16[64,7168]{1,0:T(8,128)(2,1)}, u32[]{:S(2)}, u32[]{:S(2)}) collective-permute-start(bf16[64,7168]{1,0:T(8,128)(2,1)S(1)} %bitcast.47), channel_id=1, source_target_pairs={{0,6},{1,7},{2,0},{3,1},{4,2},{5,3},{6,4},{7,5},{8,14},{9,15},{10,... | collective-permute-start | bytes 2752520 | tf_op jit(solution)/shard_map/ppermute | solution.py:486
  25.8 23.3 %collective-permute-start.3 = (bf16[48,7168]{1,0:T(8,128)(2,1)}, bf16[48,7168]{1,0:T(8,128)(2,1)}, u32[]{:S(2)}, u32[]{:S(2)}) collective-permute-start(bf16[48,7168]{1,0:T(8,128)(2,1)} %slice_bitcast_fusion), channel_id=1, source_target_pairs={{0,224},{32,0},{64,32},{96,64},{128,96},{160,128},{192,160},{224,1... | collective-permute-start | bytes 2064392 | tf_op jit(solution)/shard_map/ppermute | solution.py:491
  31.6 17.5 %all-to-all-start.1 = ((bf16[4,8,7168]{2,1,0:T(8,128)(2,1)}), bf16[4,8,7168]{2,1,0:T(8,128)(2,1)S(1)}, u32[]{:S(2)}, u32[]{:S(2)}) async-start(bf16[4,8,7168]{2,1,0:T(8,128)(2,1)} %bitcast.69), calls=%async_computation.1 | async-start | bytes 917504 | tf_op jit(solution)/shard_map/all_to_all | solution.py:501
  35.2 10.2 %collective-permute-start.4 = (f32[32,96]{1,0:T(8,128)S(1)}, f32[32,96]{1,0:T(8,128)S(1)}, u32[]{:S(2)}, u32[]{:S(2)}) collective-permute-start(f32[32,96]{1,0:T(8,128)S(1)} %fusion.9), channel_id=1, source_target_pairs={{0,32},{32,64},{64,96},{96,128},{128,160},{160,192},{192,224},{224... | collective-permute-start | bytes 36872 | tf_op jit(solution)/shard_map/ppermute | solution.py:491
  49.2 11.4 %collective-permute-start.10 = (bf16[64,7168]{1,0:T(8,128)(2,1)S(1)}, bf16[64,7168]{1,0:T(8,128)(2,1)S(1)}, u32[]{:S(2)}, u32[]{:S(2)}) collective-permute-start(bf16[64,7168]{1,0:T(8,128)(2,1)S(1)} %bitcast.48), channel_id=1, source_target_pairs={{0,1},{1,0},{2,3},{3,2},{4,5},{5,4},{6,7},{7,6},{8,9},{9,8},{10,11... | collective-permute-start | bytes 2752520 | tf_op jit(solution)/shard_map/ppermute | solution.py:486
  49.7 12.6 %collective-permute-start.11 = (bf16[64,7168]{1,0:T(8,128)(2,1)}, bf16[64,7168]{1,0:T(8,128)(2,1)S(1)}, u32[]{:S(2)}, u32[]{:S(2)}) collective-permute-start(bf16[64,7168]{1,0:T(8,128)(2,1)} %collective-permute-done.refs_1_.refs_7_), channel_id=1, source_target_pairs={{0,1},{1,0},{2,3},{3,2},{4,5},{5,4},{6,7},{7,6},{8,9},{9,8},{10,11... | collective-permute-start | bytes 2752520 | tf_op jit(solution)/shard_map/ppermute | solution.py:486
  53.4 28.7 %collective-permute-start.13 = (bf16[48,7168]{1,0:T(8,128)(2,1)S(1)}, bf16[48,7168]{1,0:T(8,128)(2,1)S(1)}, u32[]{:S(2)}, u32[]{:S(2)}) collective-permute-start(bf16[48,7168]{1,0:T(8,128)(2,1)S(1)} %slice.91), channel_id=1, source_target_pairs={{0,224},{32,0},{64,32},{96,64},{128,96},{160,128},{192,160},{224,1... | collective-permute-start | bytes 2064392 | tf_op jit(solution)/shard_map/ppermute | solution.py:491
  58.5 13.5 %collective-permute-start.6 = (bf16[32,7168]{1,0:T(8,128)(2,1)S(1)}, bf16[32,7168]{1,0:T(8,128)(2,1)S(1)}, u32[]{:S(2)}, u32[]{:S(2)}) collective-permute-start(bf16[32,7168]{1,0:T(8,128)(2,1)S(1)} %slice.89), channel_id=1, source_target_pairs={{0,2},{1,3},{2,4},{3,5},{4,6},{5,7},{6,0},{7,1},{8,10},{9,11},{10,... | collective-permute-start | bytes 1376264 | tf_op jit(solution)/shard_map/ppermute | solution.py:486
  59.1 14.7 %collective-permute-start.7 = (bf16[32,7168]{1,0:T(8,128)(2,1)S(1)}, bf16[32,7168]{1,0:T(8,128)(2,1)S(1)}, u32[]{:S(2)}, u32[]{:S(2)}) collective-permute-start(bf16[32,7168]{1,0:T(8,128)(2,1)S(1)} %slice.90), channel_id=1, source_target_pairs={{0,6},{1,7},{2,0},{3,1},{4,2},{5,3},{6,4},{7,5},{8,14},{9,15},{10,... | collective-permute-start | bytes 1376264 | tf_op jit(solution)/shard_map/ppermute | solution.py:486
  60.6 20.1 %collective-permute-start.8 = (bf16[32,7168]{1,0:T(8,128)(2,1)S(1)}, bf16[32,7168]{1,0:T(8,128)(2,1)S(1)}, u32[]{:S(2)}, u32[]{:S(2)}) collective-permute-start(bf16[32,7168]{1,0:T(8,128)(2,1)S(1)} %bitcast.52), channel_id=1, source_target_pairs={{0,2},{1,3},{2,4},{3,5},{4,6},{5,7},{6,0},{7,1},{8,10},{9,11},{10,... | collective-permute-start | bytes 1376264 | tf_op jit(solution)/shard_map/ppermute | solution.py:486
  62.3 19.8 %collective-permute-start.9 = (bf16[32,7168]{1,0:T(8,128)(2,1)S(1)}, bf16[32,7168]{1,0:T(8,128)(2,1)S(1)}, u32[]{:S(2)}, u32[]{:S(2)}) collective-permute-start(bf16[32,7168]{1,0:T(8,128)(2,1)S(1)} %bitcast.53), channel_id=1, source_target_pairs={{0,6},{1,7},{2,0},{3,1},{4,2},{5,3},{6,4},{7,5},{8,14},{9,15},{10,... | collective-permute-start | bytes 1376264 | tf_op jit(solution)/shard_map/ppermute | solution.py:486
  88.0 9.6 %collective-permute-start.16 = (bf16[128,7296]{1,0:T(8,128)(2,1)S(1)}, bf16[128,7296]{1,0:T(8,128)(2,1)S(1)}, u32[]{:S(2)}, u32[]{:S(2)}) collective-permute-start(bf16[128,7296]{1,0:T(8,128)(2,1)S(1)} %get-tuple-element.66), channel_id=1, source_target_pairs={{0,1},{1,0},{2,3},{3,2},{4,5},{5,4},{6,7},{7,6},{8,9},{9,8},{10,11... | collective-permute-start | bytes 5603336 | tf_op jit(solution)/shard_map/ppermute | solution.py:486
  88.2 8.0 %collective-permute-start.17 = (bf16[16,7168]{1,0:T(8,128)(2,1)S(1)}, bf16[16,7168]{1,0:T(8,128)(2,1)S(1)}, u32[]{:S(2)}, u32[]{:S(2)}) collective-permute-start(bf16[16,7168]{1,0:T(8,128)(2,1)S(1)} %slice.92), channel_id=1, source_target_pairs={{0,2},{1,3},{2,4},{3,5},{4,6},{5,7},{6,0},{7,1},{8,10},{9,11},{10,... | collective-permute-start | bytes 688136 | tf_op jit(solution)/shard_map/ppermute | solution.py:486
  88.7 8.9 %collective-permute-start.18 = (bf16[16,7168]{1,0:T(8,128)(2,1)S(1)}, bf16[16,7168]{1,0:T(8,128)(2,1)S(1)}, u32[]{:S(2)}, u32[]{:S(2)}) collective-permute-start(bf16[16,7168]{1,0:T(8,128)(2,1)S(1)} %slice.93), channel_id=1, source_target_pairs={{0,6},{1,7},{2,0},{3,1},{4,2},{5,3},{6,4},{7,5},{8,14},{9,15},{10,... | collective-permute-start | bytes 688136 | tf_op jit(solution)/shard_map/ppermute | solution.py:486
  90.4 8.2 %collective-permute-start.19 = (bf16[32,7168]{1,0:T(8,128)(2,1)S(1)}, bf16[32,7168]{1,0:T(8,128)(2,1)S(1)}, u32[]{:S(2)}, u32[]{:S(2)}) collective-permute-start(bf16[32,7168]{1,0:T(8,128)(2,1)S(1)} %bitcast.54), channel_id=1, source_target_pairs={{0,1},{1,0},{2,3},{3,2},{4,5},{5,4},{6,7},{7,6},{8,9},{9,8},{10,11... | collective-permute-start | bytes 1376264 | tf_op jit(solution)/shard_map/ppermute | solution.py:486
  90.4 8.5 %collective-permute-start.20 = (bf16[32,7168]{1,0:T(8,128)(2,1)S(1)}, bf16[32,7168]{1,0:T(8,128)(2,1)S(1)}, u32[]{:S(2)}, u32[]{:S(2)}) collective-permute-start(bf16[32,7168]{1,0:T(8,128)(2,1)S(1)} %collective-permute-done.8.refs_1_), channel_id=1, source_target_pairs={{0,1},{1,0},{2,3},{3,2},{4,5},{5,4},{6,7},{7,6},{8,9},{9,8},{10,11... | collective-permute-start | bytes 1376264 | tf_op jit(solution)/shard_map/ppermute | solution.py:486
  99.0 9.0 %collective-permute-start.35 = (bf16[16,7296]{1,0:T(8,128)(2,1)S(1)}, bf16[16,7296]{1,0:T(8,128)(2,1)S(1)}, u32[]{:S(2)}, u32[]{:S(2)}) collective-permute-start(bf16[16,7296]{1,0:T(8,128)(2,1)S(1)} %get-tuple-element.92), channel_id=1, source_target_pairs={{0,6},{1,7},{2,0},{3,1},{4,2},{5,3},{6,4},{7,5},{8,14},{9,15},{10,... | collective-permute-start | bytes 700424 | tf_op jit(solution)/shard_map/ppermute | solution.py:486
  108.1 19.4 %collective-permute-start.34 = (bf16[32,7296]{1,0:T(8,128)(2,1)S(1)}, bf16[32,7296]{1,0:T(8,128)(2,1)S(1)}, u32[]{:S(2)}, u32[]{:S(2)}) collective-permute-start(bf16[32,7296]{1,0:T(8,128)(2,1)S(1)} %pad_maximum_fusion), channel_id=1, source_target_pairs={{0,2},{1,3},{2,4},{3,5},{4,6},{5,7},{6,0},{7,1},{8,10},{9,11},{10,... | collective-permute-start | bytes 1400840 | tf_op jit(solution)/shard_map/ppermute | solution.py:486
  109.0 15.9 %collective-permute-start.25 = (bf16[16,7168]{1,0:T(8,128)(2,1)S(1)}, bf16[16,7168]{1,0:T(8,128)(2,1)S(1)}, u32[]{:S(2)}, u32[]{:S(2)}) collective-permute-start(bf16[16,7168]{1,0:T(8,128)(2,1)S(1)} %get-tuple-element.95), channel_id=1, source_target_pairs={{0,2},{1,3},{2,4},{3,5},{4,6},{5,7},{6,0},{7,1},{8,10},{9,11},{10,... | collective-permute-start | bytes 688136 | tf_op jit(solution)/shard_map/ppermute | solution.py:486
  110.3 14.7 %collective-permute-start.27 = (bf16[16,7168]{1,0:T(8,128)(2,1)S(1)}, bf16[16,7168]{1,0:T(8,128)(2,1)S(1)}, u32[]{:S(2)}, u32[]{:S(2)}) collective-permute-start(bf16[16,7168]{1,0:T(8,128)(2,1)S(1)} %get-tuple-element.96), channel_id=1, source_target_pairs={{0,6},{1,7},{2,0},{3,1},{4,2},{5,3},{6,4},{7,5},{8,14},{9,15},{10,... | collective-permute-start | bytes 688136 | tf_op jit(solution)/shard_map/ppermute | solution.py:486
  111.2 17.7 %collective-permute-start.36 = (bf16[32,7296]{1,0:T(8,128)(2,1)S(1)}, bf16[32,7296]{1,0:T(8,128)(2,1)S(1)}, u32[]{:S(2)}, u32[]{:S(2)}) collective-permute-start(bf16[32,7296]{1,0:T(8,128)(2,1)S(1)} %pad_maximum_fusion.1), channel_id=1, source_target_pairs={{0,6},{1,7},{2,0},{3,1},{4,2},{5,3},{6,4},{7,5},{8,14},{9,15},{10,... | collective-permute-start | bytes 1400840 | tf_op jit(solution)/shard_map/ppermute | solution.py:486
  125.1 19.0 %collective-permute-start.26 = (bf16[32,7168]{1,0:T(8,128)(2,1)S(1)}, bf16[32,7168]{1,0:T(8,128)(2,1)S(1)}, u32[]{:S(2)}, u32[]{:S(2)}) collective-permute-start(bf16[32,7168]{1,0:T(8,128)(2,1)S(1)} %pad_maximum_fusion.2), channel_id=1, source_target_pairs={{0,2},{1,3},{2,4},{3,5},{4,6},{5,7},{6,0},{7,1},{8,10},{9,11},{10,... | collective-permute-start | bytes 1376264 | tf_op jit(solution)/shard_map/ppermute | solution.py:486
  127.1 17.0 %collective-permute-start.28 = (bf16[32,7168]{1,0:T(8,128)(2,1)S(1)}, bf16[32,7168]{1,0:T(8,128)(2,1)S(1)}, u32[]{:S(2)}, u32[]{:S(2)}) collective-permute-start(bf16[32,7168]{1,0:T(8,128)(2,1)S(1)} %pad_maximum_fusion.3), channel_id=1, source_target_pairs={{0,6},{1,7},{2,0},{3,1},{4,2},{5,3},{6,4},{7,5},{8,14},{9,15},{10,... | collective-permute-start | bytes 1376264 | tf_op jit(solution)/shard_map/ppermute | solution.py:486
  129.9 12.5 %all-to-all-start.2 = ((bf16[4,8,7296]{2,1,0:T(8,128)(2,1)}), bf16[4,8,7296]{2,1,0:T(8,128)(2,1)S(1)}, u32[]{:S(2)}, u32[]{:S(2)}) async-start(bf16[4,8,7296]{2,1,0:T(8,128)(2,1)} %fusion.4), calls=%async_computation.2 | async-start | bytes 933888 | tf_op jit(solution)/shard_map/all_to_all | solution.py:501
  143.8 9.9 %collective-permute-start.37 = (bf16[32,7168]{1,0:T(8,128)(2,1)S(1)}, bf16[32,7168]{1,0:T(8,128)(2,1)S(1)}, u32[]{:S(2)}, u32[]{:S(2)}) collective-permute-start(bf16[32,7168]{1,0:T(8,128)(2,1)S(1)} %get-tuple-element.81), channel_id=1, source_target_pairs={{0,224},{32,0},{64,32},{96,64},{128,96},{160,128},{192,160},{224,1... | collective-permute-start | bytes 1376264 | tf_op jit(solution)/shard_map/ppermute | solution.py:491
  145.5 10.8 %collective-permute-start.29 = (bf16[8,7168]{1,0:T(8,128)(2,1)S(1)}, bf16[8,7168]{1,0:T(8,128)(2,1)S(1)}, u32[]{:S(2)}, u32[]{:S(2)}) collective-permute-start(bf16[8,7168]{1,0:T(8,128)(2,1)S(1)} %get-tuple-element.102), channel_id=1, source_target_pairs={{0,32},{32,64},{64,96},{96,128},{128,160},{160,192},{192,224},{224... | collective-permute-start | bytes 344072 | tf_op jit(solution)/shard_map/ppermute | solution.py:491
  147.3 9.0 %collective-permute-start.30 = (bf16[8,7168]{1,0:T(8,128)(2,1)S(1)}, bf16[8,7168]{1,0:T(8,128)(2,1)S(1)}, u32[]{:S(2)}, u32[]{:S(2)}) collective-permute-start(bf16[8,7168]{1,0:T(8,128)(2,1)S(1)} %get-tuple-element.101), channel_id=1, source_target_pairs={{0,56},{1,57},{2,58},{3,59},{4,60},{5,61},{6,62},{7,63},{8,32},{9,... | collective-permute-start | bytes 344072 | tf_op jit(solution)/shard_map/ppermute | solution.py:497
  148.1 9.3 %collective-permute-start.31 = (bf16[8,7168]{1,0:T(8,128)(2,1)S(1)}, bf16[8,7168]{1,0:T(8,128)(2,1)S(1)}, u32[]{:S(2)}, u32[]{:S(2)}) collective-permute-start(bf16[8,7168]{1,0:T(8,128)(2,1)S(1)} %get-tuple-element.100), channel_id=1, source_target_pairs={{0,48},{1,49},{2,50},{3,51},{4,52},{5,53},{6,54},{7,55},{8,56},{9,... | collective-permute-start | bytes 344072 | tf_op jit(solution)/shard_map/ppermute | solution.py:497
  148.2 10.3 %collective-permute-start.32 = (bf16[8,7168]{1,0:T(8,128)(2,1)S(1)}, bf16[8,7168]{1,0:T(8,128)(2,1)S(1)}, u32[]{:S(2)}, u32[]{:S(2)}) collective-permute-start(bf16[8,7168]{1,0:T(8,128)(2,1)S(1)} %get-tuple-element.99), channel_id=1, source_target_pairs={{0,40},{1,41},{2,42},{3,43},{4,44},{5,45},{6,46},{7,47},{8,48},{9,... | collective-permute-start | bytes 344072 | tf_op jit(solution)/shard_map/ppermute | solution.py:497
  (28 other events, 273.3 us)

commit v3 on v2

--- a/solution.py
+++ b/solution.py
@@ -96,7 +96,8 @@
     @pl.when(step == 0)
     def _():
         table, mixing, first = tables(routes_ref[...], scores_ref[...], slots)
-        first_ref[...] = first
+        first_ref[...] = jnp.zeros(first_ref.shape, f32)
+        first_ref[:, : table.shape[1]] = first
         table_ref[...] = table
         weights_ref[...] = exact(table, mixing, ((1,), (1,)))
         take_ref[...] = table.astype(bf16)
@@ -166,7 +167,7 @@
         ((2 * slots, width), bf16),
         ((slots, width), bf16),
         ((slots, width), bf16),
-        ((slots, rows), f32),
+        ((slots, LANES), f32),
         ((slots, rows), f32),
         ((slots, slots), f32),
         ((slots, LANES), f32),
@@ -380,7 +381,7 @@
 
 
 def grad_slots_kernel(
-    routes_ref, scores_ref, table_ref, weights_ref, inverse_ref, xs_ref, cs_ref, gain_ref, dn_ref,
+    routes_ref, scores_ref, table_ref, first_ref, weights_ref, inverse_ref, xs_ref, cs_ref, gain_ref, dn_ref,
     grad_ref, score_ref
 ):
     slots, width = xs_ref.shape
@@ -389,7 +390,8 @@
     inverse = inverse_ref[:, :1]
     mean = jnp.mean(x * t, axis=1, keepdims=True)
     grad = cs_ref[...].astype(f32) + inverse * t - x * (inverse * inverse * inverse * mean)
-    grad_ref[...] = grad.astype(bf16)
+    grad_ref[:, :width] = grad.astype(bf16)
+    grad_ref[:, width:] = first_ref[...].astype(bf16)
 
     routes = routes_ref[...]
     topk, rows = routes.shape
@@ -406,31 +408,51 @@
     score_ref[...] = affinity * (1.0 - affinity) * (ROUTE_SCALE / total) * (dgate - term)
 
 
-def grad_slots(routes, scores, table, weights, inverse, xs, cs, gain, dn):
+def grad_slots(routes, scores, table, first, weights, inverse, xs, cs, gain, dn):
     slots, width = xs.shape
     return pl.pallas_call(
         grad_slots_kernel,
         out_shape=[
-            jax.ShapeDtypeStruct((slots, width), bf16),
+            jax.ShapeDtypeStruct((slots, width + LANES), bf16),
             jax.ShapeDtypeStruct(scores.shape, f32),
         ],
-        in_specs=[vmem()] * 9,
+        in_specs=[vmem()] * 10,
         out_specs=[vmem()] * 2,
         compiler_params=params(),
         cost_estimate=cost(4 * slots * slots * width, 8 * slots * width),
         name="grad_slots",
-    )(routes, scores, table, weights, inverse, xs, cs, gain, dn)
+    )(routes, scores, table, first, weights, inverse, xs, cs, gain, dn)
 
 
 def stacked(refs):
     return jnp.concatenate([r[...].astype(f32) for r in refs], axis=0)
 
 
-def place_grad_kernel(first_ref, top_ref, bottom_ref, slots_ref, out_ref):
-    first = first_ref[...].astype(bf16)
+def place_grad_kernel(top_ref, bottom_ref, slots_ref, first_ref, out_ref):
+    rows = out_ref.shape[0]
+    first = first_ref[...][:, :rows]
     touched = dot(first, jnp.ones((first.shape[0], LANES), bf16), ((0,), (0,)))[:, :1]
     placed = dot(first, slots_ref[...], ((0,), (0,)))
     out_ref[...] = jnp.where(touched > 0.0, placed, stacked([top_ref, bottom_ref])).astype(bf16)
+
+
+def place_grad(early, late):
+    width = early[0].shape[1]
+    rows = sum(e.shape[0] for e in early)
+    slots = late.shape[0]
+    steps = 2
+    block = width // steps
+    return pl.pallas_call(
+        place_grad_kernel,
+        out_shape=jax.ShapeDtypeStruct((rows, width), bf16),
+        grid=(steps,),
+        in_specs=[across(e.shape[0], block) for e in early]
+        + [across(slots, block), pl.BlockSpec((slots, LANES), lambda i: (0, width // LANES))],
+        out_specs=across(rows, block),
+        compiler_params=params(),
+        cost_estimate=cost(2 * rows * slots * width, 6 * rows * width),
+        name="place_grad",
+    )(*early, late, late)
 
 
 def place_fwd_kernel(mixing_ref, early_ref, *refs):
@@ -571,9 +593,8 @@
     top_c = net.relay(cot[:middle], -1)
     mixing = block_of(jnp.concatenate([mixing, mixing], axis=0), row, CAP, window)
     mixing = net.relay(mixing, 1)
-    first = net.relay(first, -1)
-    left_b, right_b, mine_f, early_f, top_c, mixing, first = lax.optimization_barrier(
-        (left_b, right_b, mine_f, early_f, top_c, mixing, first)
+    left_b, right_b, mine_f, early_f, top_c, mixing = lax.optimization_barrier(
+        (left_b, right_b, mine_f, early_f, top_c, mixing)
     )
 
     far_b = net.far(left_b, right_b)
@@ -600,11 +621,11 @@
         for d in range(window)
     ]
     grads, score_rows = grad_slots(
-        routes_b, scores_b, table, weights, inverse, xs, cs, gain, dn
+        routes_b, scores_b, table, first, weights, inverse, xs, cs, gain, dn
     )
     late_b = net.relay(grads, -1)
     fwd_handoff = place(place_fwd_kernel, "place_fwd", mixing, (early_f,), *outs)
-    grad_handoff = place(place_grad_kernel, "place_grad", first, (top_c, bottom_c), late_b)
+    grad_handoff = place_grad((top_c, bottom_c), late_b)
     return (fwd_handoff[None], grad_handoff[None], score_rows.T[None])
 
 

time: 162 us -> 161 us (level)
    pallas_call x2 -> x1, Pallas kernels: 5.66 us -> 3.05 us  [place(): pl.pallas_call(kernel, out_shape=jax.ShapeDtypeStruct((rows, width), bf16...]
    pallas_call x0 -> x1, Pallas kernels: none -> 2.61 us  [place_grad(): pl.pallas_call(place_grad_kernel, out_shape=jax.ShapeDtypeStruct((rows, w...]
    ppermute x7 -> x6, starting transfers between devices: 14.7 us -> 16.7 us  [relay(): return lax.ppermute(array, 'section', pairs)]
    ppermute x7 -> x6, waiting for transfers between devices: 15.7 us -> 15.2 us  [relay(): return lax.ppermute(array, 'section', pairs)]
  transfers between devices with their start and end apart: 41 -> 40, of which waited for: 20 -> 19; matrix products, arithmetic and copies ran while one was open for 5% -> 5% of each run, Pallas kernels for 8% -> 8%
where the time goes in v3:
time: 161 us
  waiting for transfers between devices  75.4 us (47%)
  starting transfers between devices  49.6 us (31%)
  Pallas kernels  23.6 us (15%)
  local copies, waits for them, and re-layouts  7.47 us (5%)
  other arithmetic  3.55 us (2%)
    ppermute x28, waiting for transfers between devices, move(): return lax.ppermute(array, 'expert', self.pairs(dy, dx, dc))  41.1 us
    ppermute x28, starting transfers between devices, move(): return lax.ppermute(array, 'expert', self.pairs(dy, dx, dc))  19.8 us
    all_to_all x3, waiting for transfers between devices, exchange(): lax.all_to_all(blocks, 'expert', 0, 0, tiled=True, axis_index_groups=self...  17.1 us
    ppermute x6, starting transfers between devices, relay(): return lax.ppermute(array, 'section', pairs)  16.7 us
    ppermute x6, waiting for transfers between devices, relay(): return lax.ppermute(array, 'section', pairs)  15.2 us
    all_to_all x3, starting transfers between devices, exchange(): lax.all_to_all(blocks, 'expert', 0, 0, tiled=True, axis_index_groups=self...  11.4 us
    pallas_call x2, Pallas kernels, enter_bwd(): pl.pallas_call(functools.partial(enter_bwd_kernel, steps, len(cots)), out...  4.96 us
    pallas_call x1, Pallas kernels, prep_bwd(): pl.pallas_call(functools.partial(prep_bwd_kernel, steps), out_shape=[jax....  3.91 us
  transfers between devices with their start and end apart: 40, of which 19 were waited for; matrix products, arithmetic and copies ran while one was open for 5% of the time, Pallas kernels for 8%

profile of v3, /device:TPU:6, one launch (start us, length us, event | category | flops | bytes accessed | tf_op | source)
XLA Modules:
  0.0 160.7 jit_solution(9731920317330831936)
XLA Ops:
  0.6 3.9 %prep_bwd.1 = (bf16[64,7168]{1,0:T(8,128)(2,1)}, bf16[32,7168]{1,0:T(8,128)(2,1)}, bf16[32,7168]{1,0:T(8,128)(2,1)}, f32[32,128]{1,0:T(8,128)}, f32[32,96]{1,0:T...) custom-call(s32[8,96]{1,0:T(8,128)} %bitcast.56, f32[8,96]{1,0:T(8,128)} %bitcast.58, bf16[96,7168]{1,0:T(8,128)(2,1)} %bitcast.64, ...), custom_call_target="tpu_custom_call" | custom-call | flops 88080384 | bytes 5505024 | tf_op jit(solution)/shard_map/prep_bwd/pallas_call | solution.py:175
  4.5 4.5 %all-to-all-start = ((bf16[4,16,7168]{2,1,0:T(8,128)(2,1)}), bf16[4,16,7168]{2,1,0:T(8,128)(2,1)S(1)}, u32[]{:S(2)}, u32[]{:S(2)}) async-start(bf16[4,16,7168]{2,1,0:T(8,128)(2,1)} %bitcast.68), calls=%async_computation | async-start | bytes 1835008 | tf_op jit(solution)/shard_map/all_to_all | solution.py:523
  9.0 1.9 %collective-permute-start.2 = (bf16[96,7168]{1,0:T(8,128)(2,1)}, bf16[96,7168]{1,0:T(8,128)(2,1)}, u32[]{:S(2)}, u32[]{:S(2)}) collective-permute-start(bf16[96,7168]{1,0:T(8,128)(2,1)} %bitcast.65), channel_id=1, source_target_pairs={{0,32},{32,64},{64,96},{96,128},{128,160},{160,192},{192,224},{224... | collective-permute-start | bytes 4128776 | tf_op jit(solution)/shard_map/ppermute | solution.py:513
  10.9 2.8 %prep_fwd.1 = (bf16[32,7168]{1,0:T(8,128)(2,1)}, f32[32,96]{1,0:T(8,128)}) custom-call(s32[8,96]{1,0:T(8,128)} %bitcast.70, f32[8,96]{1,0:T(8,128)} %bitcast.71, bf16[96,7168]{1,0:T(8,128)(2,1)} %bitcast.66, f32[1,7168]{1,0:T(1,128)} %gain_ref.5), custom_call_target="tpu_custom_call" | custom-call | flops 44040192 | bytes 2752512 | tf_op jit(solution)/shard_map/prep_fwd/pallas_call | solution.py:199
  13.8 9.0 %all-to-all-done = bf16[4,16,7168]{2,1,0:T(8,128)(2,1)S(1)} async-done(((bf16[4,16,7168]{2,1,0:T(8,128)(2,1)}), bf16[4,16,7168]{2,1,0:T(8,128)(2,1)S(1)}, u32[]{:S(2)}, u32[]{:S(2)}) %all-to-all-start) | async-done | bytes 917536 | tf_op jit(solution)/shard_map/all_to_all | solution.py:523
  23.3 1.5 collective-permute-start.1
  25.8 5.8 %collective-permute-start.3 = (bf16[48,7168]{1,0:T(8,128)(2,1)}, bf16[48,7168]{1,0:T(8,128)(2,1)}, u32[]{:S(2)}, u32[]{:S(2)}) collective-permute-start(bf16[48,7168]{1,0:T(8,128)(2,1)} %slice_bitcast_fusion), channel_id=1, source_target_pairs={{0,224},{32,0},{64,32},{96,64},{128,96},{160,128},{192,160},{224,1... | collective-permute-start | bytes 2064392 | tf_op jit(solution)/shard_map/ppermute | solution.py:513
  31.6 3.5 %all-to-all-start.1 = ((bf16[4,8,7168]{2,1,0:T(8,128)(2,1)}), bf16[4,8,7168]{2,1,0:T(8,128)(2,1)S(1)}, u32[]{:S(2)}, u32[]{:S(2)}) async-start(bf16[4,8,7168]{2,1,0:T(8,128)(2,1)} %bitcast.69), calls=%async_computation.1 | async-start | bytes 917504 | tf_op jit(solution)/shard_map/all_to_all | solution.py:523
  35.3 10.1 %collective-permute-done.4.mixing_ref = f32[32,96]{1,0:T(8,128)S(1)} collective-permute-done((f32[32,96]{1,0:T(8,128)S(1)}, f32[32,96]{1,0:T(8,128)S(1)}, u32[]{:S(2)}, u32[]{:S(2)}) %collective-permute-start.4) | collective-permute-done | bytes 12320 | tf_op jit(solution)/shard_map/ppermute | solution.py:513
  46.1 2.4 %collective-permute-done.11.refs_5_.refs_11_ = bf16[64,7168]{1,0:T(8,128)(2,1)S(1)} collective-permute-done((bf16[64,7168]{1,0:T(8,128)(2,1)}, bf16[64,7168]{1,0:T(8,128)(2,1)S(1)}, u32[]{:S(2)}, u32[]{:S(2)}) %collective-permute-start.11) | collective-permute-done | bytes 917536 | tf_op jit(solution)/shard_map/ppermute | solution.py:508
  49.6 6.7 %collective-permute-start.12 = (bf16[48,7168]{1,0:T(8,128)(2,1)S(1)}, bf16[48,7168]{1,0:T(8,128)(2,1)S(1)}, u32[]{:S(2)}, u32[]{:S(2)}) collective-permute-start(bf16[48,7168]{1,0:T(8,128)(2,1)S(1)} %slice.91), channel_id=1, source_target_pairs={{0,224},{32,0},{64,32},{96,64},{128,96},{160,128},{192,160},{224,1... | collective-permute-start | bytes 2064392 | tf_op jit(solution)/shard_map/ppermute | solution.py:513
  58.8 1.7 %collective-permute-start.6 = (bf16[32,7168]{1,0:T(8,128)(2,1)S(1)}, bf16[32,7168]{1,0:T(8,128)(2,1)S(1)}, u32[]{:S(2)}, u32[]{:S(2)}) collective-permute-start(bf16[32,7168]{1,0:T(8,128)(2,1)S(1)} %slice.90), channel_id=1, source_target_pairs={{0,6},{1,7},{2,0},{3,1},{4,2},{5,3},{6,4},{7,5},{8,14},{9,15},{10,... | collective-permute-start | bytes 1376264 | tf_op jit(solution)/shard_map/ppermute | solution.py:508
  65.5 3.2 %enter_bwd.2 = (f32[192,256]{1,0:T(8,128)S(1)}, f32[192,128]{1,0:T(8,128)S(1)}) custom-call(bf16[64,7168]{1,0:T(8,128)(2,1)S(1)} %bitcast.49, bf16[64,7168]{1,0:T(8,128)(2,1)} %collective-permute-done.refs_1_.refs_7_, bf16[64,7168]{1,0:T(8,128)(2,1)} %collective-permute-done.1.refs_2_.refs_8_, bf16[64,7168]{1,0:T(8,128)(2,1)S(1)} %collective-permute-done.9.refs_3_.refs_9_, ...), custom_call_target="tpu_custom_call" | custom-call | flops 1056964608 | bytes 11010048 | tf_op jit(solution)/shard_map/enter_bwd/pallas_call | solution.py:243
  68.7 3.2 %collective-permute-done.5.refs_0_ = bf16[32,7168]{1,0:T(8,128)(2,1)S(1)} collective-permute-done((bf16[32,7168]{1,0:T(8,128)(2,1)S(1)}, bf16[32,7168]{1,0:T(8,128)(2,1)S(1)}, u32[]{:S(2)}, u32[]{:S(2)}) %collective-permute-start.5) | collective-permute-done | bytes 458784 | tf_op jit(solution)/shard_map/ppermute | solution.py:508
  71.9 1.5 collective-permute-done.6.refs_2_
  73.4 7.2 %collective-permute-done.7.refs_1_ = bf16[32,7168]{1,0:T(8,128)(2,1)S(1)} collective-permute-done((bf16[32,7168]{1,0:T(8,128)(2,1)S(1)}, bf16[32,7168]{1,0:T(8,128)(2,1)S(1)}, u32[]{:S(2)}, u32[]{:S(2)}) %collective-permute-start.7) | collective-permute-done | bytes 458784 | tf_op jit(solution)/shard_map/ppermute | solution.py:508
  84.4 1.8 %enter_bwd.3 = (f32[64,256]{1,0:T(8,128)S(1)}, f32[64,128]{1,0:T(8,128)S(1)}) custom-call(bf16[32,7168]{1,0:T(8,128)(2,1)S(1)} %collective-permute-done.5.refs_0_, bf16[32,7168]{1,0:T(8,128)(2,1)S(1)} %collective-permute-done.13.refs_1_, bf16[32,7168]{1,0:T(8,128)(2,1)S(1)} %collective-permute-done.6.refs_2_, ...), custom_call_target="tpu_custom_call" | custom-call | flops 352321536 | bytes 7340032 | tf_op jit(solution)/shard_map/enter_bwd/pallas_call | solution.py:243
  86.2 1.6 leave_bwd.1
  88.6 1.6 %collective-permute-start.17 = (bf16[16,7168]{1,0:T(8,128)(2,1)S(1)}, bf16[16,7168]{1,0:T(8,128)(2,1)S(1)}, u32[]{:S(2)}, u32[]{:S(2)}) collective-permute-start(bf16[16,7168]{1,0:T(8,128)(2,1)S(1)} %slice.93), channel_id=1, source_target_pairs={{0,6},{1,7},{2,0},{3,1},{4,2},{5,3},{6,4},{7,5},{8,14},{9,15},{10,... | collective-permute-start | bytes 688136 | tf_op jit(solution)/shard_map/ppermute | solution.py:508
  90.7 5.2 %collective-permute-done.16.refs_3_ = bf16[16,7168]{1,0:T(8,128)(2,1)S(1)} collective-permute-done((bf16[16,7168]{1,0:T(8,128)(2,1)S(1)}, bf16[16,7168]{1,0:T(8,128)(2,1)S(1)}, u32[]{:S(2)}, u32[]{:S(2)}) %collective-permute-start.16) | collective-permute-done | bytes 229408 | tf_op jit(solution)/shard_map/ppermute | solution.py:508
  98.9 1.7 %collective-permute-start.34 = (bf16[16,7296]{1,0:T(8,128)(2,1)S(1)}, bf16[16,7296]{1,0:T(8,128)(2,1)S(1)}, u32[]{:S(2)}, u32[]{:S(2)}) collective-permute-start(bf16[16,7296]{1,0:T(8,128)(2,1)S(1)} %get-tuple-element.90), channel_id=1, source_target_pairs={{0,6},{1,7},{2,0},{3,1},{4,2},{5,3},{6,4},{7,5},{8,14},{9,15},{10,... | collective-permute-start | bytes 700424 | tf_op jit(solution)/shard_map/ppermute | solution.py:508
  100.6 3.3 %expert_fwd.1 = (bf16[128,7168]{1,0:T(8,128)(2,1)S(1)}, bf16[128,7168]{1,0:T(8,128)(2,1)S(1)}) custom-call(bf16[32,7168]{1,0:T(8,128)(2,1)S(1)} %bitcast.55, bf16[32,7168]{1,0:T(8,128)(2,1)S(1)} %collective-permute-done.7.refs_1_, bf16[32,7168]{1,0:T(8,128)(2,1)S(1)} %collective-permute-done.8.refs_2_, bf16[16,7168]{1,0:T(8,128)(2,1)S(1)} %collective-permute-done.16.refs_3_, ...), custom_call_target="tpu_custom_call" | custom-call | flops 1409286144 | bytes 12845056 | tf_op jit(solution)/shard_map/expert_fwd/pallas_call | solution.py:362
  104.1 2.1 %collective-permute-done.32 = bf16[16,7296]{1,0:T(8,128)(2,1)S(1)} collective-permute-done((bf16[16,7296]{1,0:T(8,128)(2,1)S(1)}, bf16[16,7296]{1,0:T(8,128)(2,1)S(1)}, u32[]{:S(2)}, u32[]{:S(2)}) %collective-permute-start.32) | collective-permute-done | bytes 233504 | tf_op jit(solution)/shard_map/ppermute | solution.py:508
  106.2 1.6 %collective-permute-done.34 = bf16[16,7296]{1,0:T(8,128)(2,1)S(1)} collective-permute-done((bf16[16,7296]{1,0:T(8,128)(2,1)S(1)}, bf16[16,7296]{1,0:T(8,128)(2,1)S(1)}, u32[]{:S(2)}, u32[]{:S(2)}) %collective-permute-start.34) | collective-permute-done | bytes 233504 | tf_op jit(solution)/shard_map/ppermute | solution.py:508
  111.3 1.8 %collective-permute-start.35 = (bf16[32,7296]{1,0:T(8,128)(2,1)S(1)}, bf16[32,7296]{1,0:T(8,128)(2,1)S(1)}, u32[]{:S(2)}, u32[]{:S(2)}) collective-permute-start(bf16[32,7296]{1,0:T(8,128)(2,1)S(1)} %pad_maximum_fusion.1), channel_id=1, source_target_pairs={{0,6},{1,7},{2,0},{3,1},{4,2},{5,3},{6,4},{7,5},{8,14},{9,15},{10,... | collective-permute-start | bytes 1400840 | tf_op jit(solution)/shard_map/ppermute | solution.py:508
  113.1 12.0 %collective-permute-done.24 = bf16[16,7168]{1,0:T(8,128)(2,1)S(1)} collective-permute-done((bf16[16,7168]{1,0:T(8,128)(2,1)S(1)}, bf16[16,7168]{1,0:T(8,128)(2,1)S(1)}, u32[]{:S(2)}, u32[]{:S(2)}) %collective-permute-start.24) | collective-permute-done | bytes 229408 | tf_op jit(solution)/shard_map/ppermute | solution.py:508
  125.2 1.9 %collective-permute-start.25 = (bf16[32,7168]{1,0:T(8,128)(2,1)S(1)}, bf16[32,7168]{1,0:T(8,128)(2,1)S(1)}, u32[]{:S(2)}, u32[]{:S(2)}) collective-permute-start(bf16[32,7168]{1,0:T(8,128)(2,1)S(1)} %pad_maximum_fusion.2), channel_id=1, source_target_pairs={{0,2},{1,3},{2,4},{3,5},{4,6},{5,7},{6,0},{7,1},{8,10},{9,11},{10,... | collective-permute-start | bytes 1376264 | tf_op jit(solution)/shard_map/ppermute | solution.py:508
  129.5 3.5 %all-to-all-start.2 = ((bf16[4,8,7296]{2,1,0:T(8,128)(2,1)}), bf16[4,8,7296]{2,1,0:T(8,128)(2,1)S(1)}, u32[]{:S(2)}, u32[]{:S(2)}) async-start(bf16[4,8,7296]{2,1,0:T(8,128)(2,1)} %fusion.4), calls=%async_computation.2 | async-start | bytes 933888 | tf_op jit(solution)/shard_map/all_to_all | solution.py:523
  133.1 8.2 %all-to-all-done.2 = bf16[4,8,7296]{2,1,0:T(8,128)(2,1)S(1)} async-done(((bf16[4,8,7296]{2,1,0:T(8,128)(2,1)}), bf16[4,8,7296]{2,1,0:T(8,128)(2,1)S(1)}, u32[]{:S(2)}, u32[]{:S(2)}) %all-to-all-start.2) | async-done | bytes 466976 | tf_op jit(solution)/shard_map/all_to_all | solution.py:523
  148.0 5.1 %collective-permute-done.36.slots_ref.first_ref = bf16[32,7296]{1,0:T(8,128)(2,1)S(1)} collective-permute-done((bf16[32,7296]{1,0:T(8,128)(2,1)S(1)}, bf16[32,7296]{1,0:T(8,128)(2,1)S(1)}, u32[]{:S(2)}, u32[]{:S(2)}) %collective-permute-start.36) | collective-permute-done | bytes 466976 | tf_op jit(solution)/shard_map/ppermute | solution.py:513
  153.0 2.6 %place_grad.1 = bf16[96,7168]{1,0:T(8,128)(2,1)} custom-call(bf16[48,7168]{1,0:T(8,128)(2,1)} %collective-permute-done.3.top_ref, bf16[48,7168]{1,0:T(8,128)(2,1)S(1)} %copy-done.6, bf16[32,7296]{1,0:T(8,128)(2,1)S(1)} %collective-permute-done.36.slots_ref.first_ref, bf16[32,7296]{1,0:T(8,128)(2,1)S(1)} %collective-permute-done.36.slots_ref.first_ref), custom_call_target="tpu_custom_call" | custom-call | flops 44040192 | bytes 4128768 | tf_op jit(solution)/shard_map/place_grad/pallas_call | solution.py:445
  157.7 3.0 %place_fwd.1 = bf16[96,7168]{1,0:T(8,128)(2,1)} custom-call(f32[32,96]{1,0:T(8,128)S(1)} %collective-permute-done.4.mixing_ref, bf16[96,7168]{1,0:T(8,128)(2,1)} %collective-permute-done.2.early_ref, bf16[8,7168]{1,0:T(8,128)(2,1)S(1)} %collective-permute-done.28.refs_0_, bf16[8,7168]{1,0:T(8,128)(2,1)S(1)} %collective-permute-done.29.refs_1_, ...), custom_call_target="tpu_custom_call" | custom-call | flops 88080384 | bytes 4128768 | tf_op jit(solution)/shard_map/place_fwd/pallas_call | solution.py:473
  (116 shorter events, 33.6 us)
Async XLA Ops:
  4.5 18.2 %all-to-all-start = ((bf16[4,16,7168]{2,1,0:T(8,128)(2,1)}), bf16[4,16,7168]{2,1,0:T(8,128)(2,1)S(1)}, u32[]{:S(2)}, u32[]{:S(2)}) async-start(bf16[4,16,7168]{2,1,0:T(8,128)(2,1)} %bitcast.68), calls=%async_computation | async-start | bytes 1835008 | tf_op jit(solution)/shard_map/all_to_all | solution.py:523
  9.0 36.3 %collective-permute-start.2 = (bf16[96,7168]{1,0:T(8,128)(2,1)}, bf16[96,7168]{1,0:T(8,128)(2,1)}, u32[]{:S(2)}, u32[]{:S(2)}) collective-permute-start(bf16[96,7168]{1,0:T(8,128)(2,1)} %bitcast.65), channel_id=1, source_target_pairs={{0,32},{32,64},{64,96},{96,128},{128,160},{160,192},{192,224},{224... | collective-permute-start | bytes 4128776 | tf_op jit(solution)/shard_map/ppermute | solution.py:513
  22.8 22.6 %collective-permute-start = (bf16[64,7168]{1,0:T(8,128)(2,1)S(1)}, bf16[64,7168]{1,0:T(8,128)(2,1)}, u32[]{:S(2)}, u32[]{:S(2)}) collective-permute-start(bf16[64,7168]{1,0:T(8,128)(2,1)S(1)} %bitcast.46), channel_id=1, source_target_pairs={{0,2},{1,3},{2,4},{3,5},{4,6},{5,7},{6,0},{7,1},{8,10},{9,11},{10,... | collective-permute-start | bytes 2752520 | tf_op jit(solution)/shard_map/ppermute | solution.py:508
  23.3 22.0 %collective-permute-start.1 = (bf16[64,7168]{1,0:T(8,128)(2,1)S(1)}, bf16[64,7168]{1,0:T(8,128)(2,1)}, u32[]{:S(2)}, u32[]{:S(2)}) collective-permute-start(bf16[64,7168]{1,0:T(8,128)(2,1)S(1)} %bitcast.47), channel_id=1, source_target_pairs={{0,6},{1,7},{2,0},{3,1},{4,2},{5,3},{6,4},{7,5},{8,14},{9,15},{10,... | collective-permute-start | bytes 2752520 | tf_op jit(solution)/shard_map/ppermute | solution.py:508
  25.8 19.6 %collective-permute-start.3 = (bf16[48,7168]{1,0:T(8,128)(2,1)}, bf16[48,7168]{1,0:T(8,128)(2,1)}, u32[]{:S(2)}, u32[]{:S(2)}) collective-permute-start(bf16[48,7168]{1,0:T(8,128)(2,1)} %slice_bitcast_fusion), channel_id=1, source_target_pairs={{0,224},{32,0},{64,32},{96,64},{128,96},{160,128},{192,160},{224,1... | collective-permute-start | bytes 2064392 | tf_op jit(solution)/shard_map/ppermute | solution.py:513
  31.6 13.7 %all-to-all-start.1 = ((bf16[4,8,7168]{2,1,0:T(8,128)(2,1)}), bf16[4,8,7168]{2,1,0:T(8,128)(2,1)S(1)}, u32[]{:S(2)}, u32[]{:S(2)}) async-start(bf16[4,8,7168]{2,1,0:T(8,128)(2,1)} %bitcast.69), calls=%async_computation.1 | async-start | bytes 917504 | tf_op jit(solution)/shard_map/all_to_all | solution.py:523
  35.2 10.2 %collective-permute-start.4 = (f32[32,96]{1,0:T(8,128)S(1)}, f32[32,96]{1,0:T(8,128)S(1)}, u32[]{:S(2)}, u32[]{:S(2)}) collective-permute-start(f32[32,96]{1,0:T(8,128)S(1)} %fusion.9), channel_id=1, source_target_pairs={{0,32},{32,64},{64,96},{96,128},{128,160},{160,192},{192,224},{224... | collective-permute-start | bytes 36872 | tf_op jit(solution)/shard_map/ppermute | solution.py:513
  45.5 15.0 %collective-permute-start.9 = (bf16[64,7168]{1,0:T(8,128)(2,1)S(1)}, bf16[64,7168]{1,0:T(8,128)(2,1)S(1)}, u32[]{:S(2)}, u32[]{:S(2)}) collective-permute-start(bf16[64,7168]{1,0:T(8,128)(2,1)S(1)} %bitcast.48), channel_id=1, source_target_pairs={{0,1},{1,0},{2,3},{3,2},{4,5},{5,4},{6,7},{7,6},{8,9},{9,8},{10,11... | collective-permute-start | bytes 2752520 | tf_op jit(solution)/shard_map/ppermute | solution.py:508
  46.0 16.0 %collective-permute-start.10 = (bf16[64,7168]{1,0:T(8,128)(2,1)}, bf16[64,7168]{1,0:T(8,128)(2,1)S(1)}, u32[]{:S(2)}, u32[]{:S(2)}) collective-permute-start(bf16[64,7168]{1,0:T(8,128)(2,1)} %collective-permute-done.refs_1_.refs_7_), channel_id=1, source_target_pairs={{0,1},{1,0},{2,3},{3,2},{4,5},{5,4},{6,7},{7,6},{8,9},{9,8},{10,11... | collective-permute-start | bytes 2752520 | tf_op jit(solution)/shard_map/ppermute | solution.py:508
  49.6 32.3 %collective-permute-start.12 = (bf16[48,7168]{1,0:T(8,128)(2,1)S(1)}, bf16[48,7168]{1,0:T(8,128)(2,1)S(1)}, u32[]{:S(2)}, u32[]{:S(2)}) collective-permute-start(bf16[48,7168]{1,0:T(8,128)(2,1)S(1)} %slice.91), channel_id=1, source_target_pairs={{0,224},{32,0},{64,32},{96,64},{128,96},{160,128},{192,160},{224,1... | collective-permute-start | bytes 2064392 | tf_op jit(solution)/shard_map/ppermute | solution.py:513
  58.4 13.5 %collective-permute-start.5 = (bf16[32,7168]{1,0:T(8,128)(2,1)S(1)}, bf16[32,7168]{1,0:T(8,128)(2,1)S(1)}, u32[]{:S(2)}, u32[]{:S(2)}) collective-permute-start(bf16[32,7168]{1,0:T(8,128)(2,1)S(1)} %slice.89), channel_id=1, source_target_pairs={{0,2},{1,3},{2,4},{3,5},{4,6},{5,7},{6,0},{7,1},{8,10},{9,11},{10,... | collective-permute-start | bytes 1376264 | tf_op jit(solution)/shard_map/ppermute | solution.py:508
  58.8 14.6 %collective-permute-start.6 = (bf16[32,7168]{1,0:T(8,128)(2,1)S(1)}, bf16[32,7168]{1,0:T(8,128)(2,1)S(1)}, u32[]{:S(2)}, u32[]{:S(2)}) collective-permute-start(bf16[32,7168]{1,0:T(8,128)(2,1)S(1)} %slice.90), channel_id=1, source_target_pairs={{0,6},{1,7},{2,0},{3,1},{4,2},{5,3},{6,4},{7,5},{8,14},{9,15},{10,... | collective-permute-start | bytes 1376264 | tf_op jit(solution)/shard_map/ppermute | solution.py:508
  60.5 20.1 %collective-permute-start.7 = (bf16[32,7168]{1,0:T(8,128)(2,1)S(1)}, bf16[32,7168]{1,0:T(8,128)(2,1)S(1)}, u32[]{:S(2)}, u32[]{:S(2)}) collective-permute-start(bf16[32,7168]{1,0:T(8,128)(2,1)S(1)} %bitcast.52), channel_id=1, source_target_pairs={{0,2},{1,3},{2,4},{3,5},{4,6},{5,7},{6,0},{7,1},{8,10},{9,11},{10,... | collective-permute-start | bytes 1376264 | tf_op jit(solution)/shard_map/ppermute | solution.py:508
  62.0 19.9 %collective-permute-start.8 = (bf16[32,7168]{1,0:T(8,128)(2,1)S(1)}, bf16[32,7168]{1,0:T(8,128)(2,1)S(1)}, u32[]{:S(2)}, u32[]{:S(2)}) collective-permute-start(bf16[32,7168]{1,0:T(8,128)(2,1)S(1)} %bitcast.53), channel_id=1, source_target_pairs={{0,6},{1,7},{2,0},{3,1},{4,2},{5,3},{6,4},{7,5},{8,14},{9,15},{10,... | collective-permute-start | bytes 1376264 | tf_op jit(solution)/shard_map/ppermute | solution.py:508
  87.8 9.7 %collective-permute-start.15 = (bf16[128,7296]{1,0:T(8,128)(2,1)S(1)}, bf16[128,7296]{1,0:T(8,128)(2,1)S(1)}, u32[]{:S(2)}, u32[]{:S(2)}) collective-permute-start(bf16[128,7296]{1,0:T(8,128)(2,1)S(1)} %get-tuple-element.64), channel_id=1, source_target_pairs={{0,1},{1,0},{2,3},{3,2},{4,5},{5,4},{6,7},{7,6},{8,9},{9,8},{10,11... | collective-permute-start | bytes 5603336 | tf_op jit(solution)/shard_map/ppermute | solution.py:508
  88.0 8.0 %collective-permute-start.16 = (bf16[16,7168]{1,0:T(8,128)(2,1)S(1)}, bf16[16,7168]{1,0:T(8,128)(2,1)S(1)}, u32[]{:S(2)}, u32[]{:S(2)}) collective-permute-start(bf16[16,7168]{1,0:T(8,128)(2,1)S(1)} %slice.92), channel_id=1, source_target_pairs={{0,2},{1,3},{2,4},{3,5},{4,6},{5,7},{6,0},{7,1},{8,10},{9,11},{10,... | collective-permute-start | bytes 688136 | tf_op jit(solution)/shard_map/ppermute | solution.py:508
  88.6 8.9 %collective-permute-start.17 = (bf16[16,7168]{1,0:T(8,128)(2,1)S(1)}, bf16[16,7168]{1,0:T(8,128)(2,1)S(1)}, u32[]{:S(2)}, u32[]{:S(2)}) collective-permute-start(bf16[16,7168]{1,0:T(8,128)(2,1)S(1)} %slice.93), channel_id=1, source_target_pairs={{0,6},{1,7},{2,0},{3,1},{4,2},{5,3},{6,4},{7,5},{8,14},{9,15},{10,... | collective-permute-start | bytes 688136 | tf_op jit(solution)/shard_map/ppermute | solution.py:508
  90.2 8.3 %collective-permute-start.18 = (bf16[32,7168]{1,0:T(8,128)(2,1)S(1)}, bf16[32,7168]{1,0:T(8,128)(2,1)S(1)}, u32[]{:S(2)}, u32[]{:S(2)}) collective-permute-start(bf16[32,7168]{1,0:T(8,128)(2,1)S(1)} %bitcast.54), channel_id=1, source_target_pairs={{0,1},{1,0},{2,3},{3,2},{4,5},{5,4},{6,7},{7,6},{8,9},{9,8},{10,11... | collective-permute-start | bytes 1376264 | tf_op jit(solution)/shard_map/ppermute | solution.py:508
  90.2 8.6 %collective-permute-start.19 = (bf16[32,7168]{1,0:T(8,128)(2,1)S(1)}, bf16[32,7168]{1,0:T(8,128)(2,1)S(1)}, u32[]{:S(2)}, u32[]{:S(2)}) collective-permute-start(bf16[32,7168]{1,0:T(8,128)(2,1)S(1)} %collective-permute-done.7.refs_1_), channel_id=1, source_target_pairs={{0,1},{1,0},{2,3},{3,2},{4,5},{5,4},{6,7},{7,6},{8,9},{9,8},{10,11... | collective-permute-start | bytes 1376264 | tf_op jit(solution)/shard_map/ppermute | solution.py:508
  98.9 9.0 %collective-permute-start.34 = (bf16[16,7296]{1,0:T(8,128)(2,1)S(1)}, bf16[16,7296]{1,0:T(8,128)(2,1)S(1)}, u32[]{:S(2)}, u32[]{:S(2)}) collective-permute-start(bf16[16,7296]{1,0:T(8,128)(2,1)S(1)} %get-tuple-element.90), channel_id=1, source_target_pairs={{0,6},{1,7},{2,0},{3,1},{4,2},{5,3},{6,4},{7,5},{8,14},{9,15},{10,... | collective-permute-start | bytes 700424 | tf_op jit(solution)/shard_map/ppermute | solution.py:508
  108.0 19.6 %collective-permute-start.33 = (bf16[32,7296]{1,0:T(8,128)(2,1)S(1)}, bf16[32,7296]{1,0:T(8,128)(2,1)S(1)}, u32[]{:S(2)}, u32[]{:S(2)}) collective-permute-start(bf16[32,7296]{1,0:T(8,128)(2,1)S(1)} %pad_maximum_fusion), channel_id=1, source_target_pairs={{0,2},{1,3},{2,4},{3,5},{4,6},{5,7},{6,0},{7,1},{8,10},{9,11},{10,... | collective-permute-start | bytes 1400840 | tf_op jit(solution)/shard_map/ppermute | solution.py:508
  109.2 15.9 %collective-permute-start.24 = (bf16[16,7168]{1,0:T(8,128)(2,1)S(1)}, bf16[16,7168]{1,0:T(8,128)(2,1)S(1)}, u32[]{:S(2)}, u32[]{:S(2)}) collective-permute-start(bf16[16,7168]{1,0:T(8,128)(2,1)S(1)} %get-tuple-element.93), channel_id=1, source_target_pairs={{0,2},{1,3},{2,4},{3,5},{4,6},{5,7},{6,0},{7,1},{8,10},{9,11},{10,... | collective-permute-start | bytes 688136 | tf_op jit(solution)/shard_map/ppermute | solution.py:508
  110.0 15.1 %collective-permute-start.26 = (bf16[16,7168]{1,0:T(8,128)(2,1)S(1)}, bf16[16,7168]{1,0:T(8,128)(2,1)S(1)}, u32[]{:S(2)}, u32[]{:S(2)}) collective-permute-start(bf16[16,7168]{1,0:T(8,128)(2,1)S(1)} %get-tuple-element.94), channel_id=1, source_target_pairs={{0,6},{1,7},{2,0},{3,1},{4,2},{5,3},{6,4},{7,5},{8,14},{9,15},{10,... | collective-permute-start | bytes 688136 | tf_op jit(solution)/shard_map/ppermute | solution.py:508
  111.3 17.3 %collective-permute-start.35 = (bf16[32,7296]{1,0:T(8,128)(2,1)S(1)}, bf16[32,7296]{1,0:T(8,128)(2,1)S(1)}, u32[]{:S(2)}, u32[]{:S(2)}) collective-permute-start(bf16[32,7296]{1,0:T(8,128)(2,1)S(1)} %pad_maximum_fusion.1), channel_id=1, source_target_pairs={{0,6},{1,7},{2,0},{3,1},{4,2},{5,3},{6,4},{7,5},{8,14},{9,15},{10,... | collective-permute-start | bytes 1400840 | tf_op jit(solution)/shard_map/ppermute | solution.py:508
  125.2 18.5 %collective-permute-start.25 = (bf16[32,7168]{1,0:T(8,128)(2,1)S(1)}, bf16[32,7168]{1,0:T(8,128)(2,1)S(1)}, u32[]{:S(2)}, u32[]{:S(2)}) collective-permute-start(bf16[32,7168]{1,0:T(8,128)(2,1)S(1)} %pad_maximum_fusion.2), channel_id=1, source_target_pairs={{0,2},{1,3},{2,4},{3,5},{4,6},{5,7},{6,0},{7,1},{8,10},{9,11},{10,... | collective-permute-start | bytes 1376264 | tf_op jit(solution)/shard_map/ppermute | solution.py:508
  127.3 16.5 %collective-permute-start.27 = (bf16[32,7168]{1,0:T(8,128)(2,1)S(1)}, bf16[32,7168]{1,0:T(8,128)(2,1)S(1)}, u32[]{:S(2)}, u32[]{:S(2)}) collective-permute-start(bf16[32,7168]{1,0:T(8,128)(2,1)S(1)} %pad_maximum_fusion.3), channel_id=1, source_target_pairs={{0,6},{1,7},{2,0},{3,1},{4,2},{5,3},{6,4},{7,5},{8,14},{9,15},{10,... | collective-permute-start | bytes 1376264 | tf_op jit(solution)/shard_map/ppermute | solution.py:508
  129.5 11.7 %all-to-all-start.2 = ((bf16[4,8,7296]{2,1,0:T(8,128)(2,1)}), bf16[4,8,7296]{2,1,0:T(8,128)(2,1)S(1)}, u32[]{:S(2)}, u32[]{:S(2)}) async-start(bf16[4,8,7296]{2,1,0:T(8,128)(2,1)} %fusion.4), calls=%async_computation.2 | async-start | bytes 933888 | tf_op jit(solution)/shard_map/all_to_all | solution.py:523
  142.7 10.4 %collective-permute-start.36 = (bf16[32,7296]{1,0:T(8,128)(2,1)S(1)}, bf16[32,7296]{1,0:T(8,128)(2,1)S(1)}, u32[]{:S(2)}, u32[]{:S(2)}) collective-permute-start(bf16[32,7296]{1,0:T(8,128)(2,1)S(1)} %get-tuple-element.79), channel_id=1, source_target_pairs={{0,224},{32,0},{64,32},{96,64},{128,96},{160,128},{192,160},{224,1... | collective-permute-start | bytes 1400840 | tf_op jit(solution)/shard_map/ppermute | solution.py:513
  145.1 10.5 %collective-permute-start.28 = (bf16[8,7168]{1,0:T(8,128)(2,1)S(1)}, bf16[8,7168]{1,0:T(8,128)(2,1)S(1)}, u32[]{:S(2)}, u32[]{:S(2)}) collective-permute-start(bf16[8,7168]{1,0:T(8,128)(2,1)S(1)} %get-tuple-element.100), channel_id=1, source_target_pairs={{0,32},{32,64},{64,96},{96,128},{128,160},{160,192},{192,224},{224... | collective-permute-start | bytes 344072 | tf_op jit(solution)/shard_map/ppermute | solution.py:513
  146.2 9.5 %collective-permute-start.29 = (bf16[8,7168]{1,0:T(8,128)(2,1)S(1)}, bf16[8,7168]{1,0:T(8,128)(2,1)S(1)}, u32[]{:S(2)}, u32[]{:S(2)}) collective-permute-start(bf16[8,7168]{1,0:T(8,128)(2,1)S(1)} %get-tuple-element.99), channel_id=1, source_target_pairs={{0,56},{1,57},{2,58},{3,59},{4,60},{5,61},{6,62},{7,63},{8,32},{9,... | collective-permute-start | bytes 344072 | tf_op jit(solution)/shard_map/ppermute | solution.py:519
  146.9 9.5 %collective-permute-start.30 = (bf16[8,7168]{1,0:T(8,128)(2,1)S(1)}, bf16[8,7168]{1,0:T(8,128)(2,1)S(1)}, u32[]{:S(2)}, u32[]{:S(2)}) collective-permute-start(bf16[8,7168]{1,0:T(8,128)(2,1)S(1)} %get-tuple-element.98), channel_id=1, source_target_pairs={{0,48},{1,49},{2,50},{3,51},{4,52},{5,53},{6,54},{7,55},{8,56},{9,... | collective-permute-start | bytes 344072 | tf_op jit(solution)/shard_map/ppermute | solution.py:519
  146.9 10.8 %collective-permute-start.31 = (bf16[8,7168]{1,0:T(8,128)(2,1)S(1)}, bf16[8,7168]{1,0:T(8,128)(2,1)S(1)}, u32[]{:S(2)}, u32[]{:S(2)}) collective-permute-start(bf16[8,7168]{1,0:T(8,128)(2,1)S(1)} %get-tuple-element.97), channel_id=1, source_target_pairs={{0,40},{1,41},{2,42},{3,43},{4,44},{5,45},{6,46},{7,47},{8,48},{9,... | collective-permute-start | bytes 344072 | tf_op jit(solution)/shard_map/ppermute | solution.py:519
  (27 other events, 251.6 us)
